TPU v7x, 256 devices: a whole 4x4x8 slice. The times are simulated.
256 devices in a mesh: tile: 16 (over x, y), mem: 16 (over z, core).
Axes of the slice: x: 4, y: 4, z: 8, core: 2. Of those that a mesh axis runs over, the one named last changes fastest.
Arguments:
- background_draws: float32 [64, 512, 1024], P('mem', 'tile'), may hold values from -6 to 6
- scaled_residuals: bfloat16 [64, 512, 1024], P('mem', 'tile'), may hold values from -6 to 6
- soil_site_tallies: int32 [16], P('tile'), may hold values from 1 to 4096, 40960 in all
- adjacent_patches: int32 [512, 9], P(('tile', 'mem')), may hold values from 0 to 512, as said below
- position_kinds: int32 [512, 9], P(('tile', 'mem')), may hold values from 0 to 8, as said below
Outputs:
- analysis: float32 [64, 512, 1024], P('mem', 'tile')
Inputs may be any that keep to these rules, and one draw needn't show every extreme that they name: `adjacent_patches`: blocks form a grid of 64 rows by 8 columns, block id = row * 8 + column. Row b of neighbours lists distinct blocks among the 3 x 3 blocks around block b inside the grid, b itself always among them; the listed entries come first and the remaining slots hold 512. position_kinds[b, s] = 3 (dr + 1) + (dc + 1) where adjacent_patches[b, s] lies dr rows and dc columns from b; 4 in slots holding 512.
All inputs are finite; a program needn't handle non-finite values. No bound on the sum of `soil_site_tallies` on one device may be relied on, other than what follows from the above.
Results may differ from a plain program's by a relative error of at most 0.0039.
Values may be sent and summed in bfloat16 or wider, within the bound.
A program may use at most 64 MiB of HBM per device.

v0:
```python
import jax
import jax.numpy as jnp
from jax import lax
from jax.sharding import PartitionSpec as P

VARS = 8
BCELL = 128
CELL_COLS = 16
GC_HALF = 2
NB = 9
BCOLS = 8


def shifted(array, axis, by):
    size = lax.axis_size(axis)
    pairs = [(i, i + by) for i in range(size) if 0 <= i + by < size]
    return lax.ppermute(array, axis, pairs)


def taper_table(block_cells, cell_cols, half_cells):
    rows_block = block_cells // cell_cols
    half_width = float(half_cells)
    cell_ids = jnp.arange(block_cells)
    cell_row = (cell_ids // cell_cols).astype(jnp.float32)
    cell_col = (cell_ids % cell_cols).astype(jnp.float32)
    class_ids = jnp.arange(9)
    shift_rows = (class_ids // 3 - 1).astype(jnp.float32) * rows_block
    shift_cols = (class_ids % 3 - 1).astype(jnp.float32) * cell_cols
    delta_rows = shift_rows[:, None, None] + cell_row[None, None, :] - cell_row[None, :, None]
    delta_cols = shift_cols[:, None, None] + cell_col[None, None, :] - cell_col[None, :, None]
    scaled = jnp.sqrt(delta_rows * delta_rows + delta_cols * delta_cols) / half_width
    near_part = (
        ((-0.25 * scaled + 0.5) * scaled + 0.625) * scaled - 5.0 / 3.0
    ) * scaled * scaled + 1.0
    safe_scaled = jnp.maximum(scaled, 1.0)
    far_part = (
        ((((scaled / 12.0 - 0.5) * scaled + 0.625) * scaled + 5.0 / 3.0) * scaled - 5.0) * scaled
        + 4.0
        - 2.0 / (3.0 * safe_scaled)
    )
    return jnp.where(scaled <= 1.0, near_part, jnp.where(scaled < 2.0, far_part, 0.0))


def direct_piece(stacked, offset_value):
    return shifted(stacked, ("tile", "mem"), offset_value)


def owner_lookup(adjacent_patches, device_pos, per_device, offsets, total_blocks):
    priority = [4, 3, 5, 1, 0, 2, 7, 6, 8]
    ordered_offsets = [offsets[slot_number] for slot_number in priority]
    owner_gap = device_pos - adjacent_patches // per_device
    matches = owner_gap[..., None] == jnp.array(ordered_offsets, jnp.int32)
    first_match = jnp.argmax(matches, axis=-1)
    slot_pos = jnp.take(jnp.array(priority, jnp.int32), first_match)
    return jnp.where(
        adjacent_patches == total_blocks,
        len(offsets) * per_device,
        slot_pos * per_device + adjacent_patches % per_device,
    )


def local(background_draws, scaled_residuals, soil_site_tallies, adjacent_patches, position_kinds):
    nearby_realizations, domain_patch_lines, patch_line_length = background_draws.shape
    mem_count = lax.axis_size("mem")
    per_device = domain_patch_lines // mem_count
    every_trial_index = nearby_realizations * mem_count
    tile_pos = lax.axis_index("tile")
    mem_pos = lax.axis_index("mem")
    total_blocks = lax.axis_size("tile") * domain_patch_lines
    cell_in = jnp.arange(patch_line_length, dtype=jnp.int32) % BCELL
    land_count = soil_site_tallies[0]
    trial_neighbourhood_arrays = lax.all_to_all(
        background_draws, "mem", split_axis=1, concat_axis=0, tiled=True
    )
    innov_blocks = lax.all_to_all(scaled_residuals, "mem", split_axis=1, concat_axis=0, tiled=True)
    expected_background_profile = jnp.sum(trial_neighbourhood_arrays, axis=0) / every_trial_index
    local_ids = mem_pos * per_device + jnp.arange(per_device, dtype=jnp.int32)
    ground_point_indicators = local_ids[:, None] * BCELL + cell_in[None, :] < land_count
    trial_departures = jnp.where(
        ground_point_indicators[None],
        trial_neighbourhood_arrays - expected_background_profile[None],
        0.0,
    ).astype(jnp.bfloat16)
    stacked = jnp.stack([trial_departures, innov_blocks])
    row_reach = max(1, BCOLS // per_device)
    offsets = [
        row_reach + 1,
        row_reach,
        row_reach - 1,
        1,
        0,
        -1,
        1 - row_reach,
        -row_reach,
        -row_reach - 1,
    ]
    device_pos = tile_pos * mem_count + mem_pos
    pieces = [
        stacked if offset_value == 0 else direct_piece(stacked, offset_value)
        for offset_value in offsets
    ]
    gathered = jnp.concatenate(pieces, axis=2)
    located = owner_lookup(adjacent_patches, device_pos, per_device, offsets, total_blocks)
    extended = jnp.concatenate(
        [gathered, jnp.zeros((2, every_trial_index, 1, patch_line_length), jnp.bfloat16)], axis=2
    )
    taper = taper_table(BCELL, CELL_COLS, GC_HALF)

    def update_block(block_index, results):
        own_block = lax.dynamic_index_in_dim(trial_departures, block_index, 1, keepdims=False)

        def add_slot(slot_index, running):
            position = located[block_index, slot_index]
            taper_kind = position_kinds[block_index, slot_index]
            far_block = lax.dynamic_index_in_dim(extended, position, 2, keepdims=False)
            covariance = lax.dot_general(
                own_block,
                far_block[0],
                (((0,), (0,)), ((), ())),
                preferred_element_type=jnp.float32,
            )
            weights = taper[taper_kind]
            shaped = covariance.reshape(VARS, BCELL, VARS, BCELL) * weights[None, :, None, :]
            tapered = (
                shaped.reshape(patch_line_length, patch_line_length) / (every_trial_index - 1)
            ).astype(jnp.bfloat16)
            return running + lax.dot_general(
                far_block[1], tapered, (((1,), (1,)), ((), ())), preferred_element_type=jnp.float32
            )

        running = lax.fori_loop(
            0, NB, add_slot, jnp.zeros((every_trial_index, patch_line_length), jnp.float32)
        )
        return lax.dynamic_update_index_in_dim(
            results, running.astype(jnp.bfloat16), block_index, 1
        )

    correction_vectors = lax.fori_loop(
        0,
        per_device,
        update_block,
        jnp.zeros((every_trial_index, per_device, patch_line_length), jnp.bfloat16),
    )
    posterior_result = lax.all_to_all(
        correction_vectors, "mem", split_axis=0, concat_axis=1, tiled=True
    )
    return background_draws + posterior_result.astype(jnp.float32)


def solution(mesh):
    in_specs = (
        P("mem", "tile", None),
        P("mem", "tile", None),
        P("tile"),
        P(("tile", "mem"), None),
        P(("tile", "mem"), None),
    )
    out_specs = P("mem", "tile", None)
    return jax.shard_map(local, mesh=mesh, in_specs=in_specs, out_specs=out_specs, check_vma=False)
```

profile of v0, /device:TPU:31, one launch (start us, length us, event | category | flops | bytes accessed | tf_op | source)
XLA Modules:
  0.0 386.2 jit_solution(5552966431434328831)
XLA Ops:
  1.9 9.2 %all-to-all-start.1 = ((bf16[4,32,1024]{2,0,1:T(4,128)(2,1)}), bf16[4,32,1024]{2,0,1:T(4,128)(2,1)S(1)}, u32[]{:S(2)}, u32[]{:S(2)}) async-start(bf16[4,32,1024]{2,0,1:T(4,128)(2,1)} %copy.49), calls=%async_computation.1 | async-start | bytes 524288 | tf_op jit(solution)/shard_map/all_to_all | solution.py:75
  16.5 6.2 %all-to-all-done.1 = bf16[4,32,1024]{2,0,1:T(4,128)(2,1)S(1)} async-done(((bf16[4,32,1024]{2,0,1:T(4,128)(2,1)}), bf16[4,32,1024]{2,0,1:T(4,128)(2,1)S(1)}, u32[]{:S(2)}, u32[]{:S(2)}) %all-to-all-start.1) | async-done | bytes 262176 | tf_op jit(solution)/shard_map/all_to_all | solution.py:75
  22.7 3.5 all-to-all-start
  26.6 16.4 %all-to-all-done = f32[4,32,1024]{2,0,1:T(4,128)S(1)} async-done(((f32[4,32,1024]{2,0,1:T(4,128)}), f32[4,32,1024]{2,0,1:T(4,128)S(1)}, u32[]{:S(2)}, u32[]{:S(2)}) %all-to-all-start) | async-done | bytes 524320 | tf_op jit(solution)/shard_map/all_to_all | solution.py:72
  43.5 3.1 collective-permute-start
  47.4 3.2 collective-permute-start.1
  50.5 2.7 collective-permute-start.2
  55.4 2.4 collective-permute-start.4
  57.9 19.0 %collective-permute-done = bf16[2,64,2,1024]{3,1,2,0:T(8,128)(2,1)} collective-permute-done((bf16[2,64,2,1024]{3,1,2,0:T(8,128)(2,1)S(1)}, bf16[2,64,2,1024]{3,1,2,0:T(8,128)(2,1)}, u32[]{:S(2)}, u32[]{:S(2)}) %collective-permute-start) | collective-permute-done | bytes 524320 | tf_op jit(solution)/shard_map/ppermute | solution.py:17
  79.9 9.1 %collective-permute-done.1 = bf16[2,64,2,1024]{3,1,2,0:T(8,128)(2,1)} collective-permute-done((bf16[2,64,2,1024]{3,1,2,0:T(8,128)(2,1)S(1)}, bf16[2,64,2,1024]{3,1,2,0:T(8,128)(2,1)}, u32[]{:S(2)}, u32[]{:S(2)}) %collective-permute-start.1) | collective-permute-done | bytes 524320 | tf_op jit(solution)/shard_map/ppermute | solution.py:17
  89.0 2.8 collective-permute-start.6
  93.0 22.5 %collective-permute-done.2 = bf16[2,64,2,1024]{3,1,2,0:T(8,128)(2,1)S(1)} collective-permute-done((bf16[2,64,2,1024]{3,1,2,0:T(8,128)(2,1)S(1)}, bf16[2,64,2,1024]{3,1,2,0:T(8,128)(2,1)S(1)}, u32[]{:S(2)}, u32[]{:S(2)}) %collective-permute-start.2) | collective-permute-done | bytes 524320 | tf_op jit(solution)/shard_map/ppermute | solution.py:17
  115.5 2.8 collective-permute-start.7
  118.6 37.5 %collective-permute-done.7 = bf16[2,64,2,1024]{3,1,2,0:T(8,128)(2,1)S(1)} collective-permute-done((bf16[2,64,2,1024]{3,1,2,0:T(8,128)(2,1)S(1)}, bf16[2,64,2,1024]{3,1,2,0:T(8,128)(2,1)S(1)}, u32[]{:S(2)}, u32[]{:S(2)}) %collective-permute-start.7) | collective-permute-done | bytes 524320 | tf_op jit(solution)/shard_map/ppermute | solution.py:17
  158.4 205.8 %while.43 = (s32[]{:T(128)}, bf16[64,2,1024]{2,0,1:T(8,128)(2,1)S(1)}, bf16[64,2,1024]{2,0,1:T(8,128)(2,1)S(1)}, s32[2,9]{1,0:T(2,128)S(1)}, bf16[2,64,19,1024]{...) while((s32[]{:T(128)}, ...), condition=%wide.region_5.6_spmd.clone, body=%wide.region_2.5_spmd.clone.sunk | while | flops 276643840 | bytes 10891807 | solution.py:138
  159.3 102.0 %while.44 = (s32[]{:T(128)}, f32[64,1024]{1,0:T(8,128)S(1)}, s32[2,9]{1,0:T(2,128)S(1)}, s32[]{:T(128)}, bf16[2,64,19,1024]{3,1,2,0:T(8,128)(2,1)}, /*index=5*/b...) while((s32[]{:T(128)}, f32[64,1024]{1,0:T(8,128)S(1)}, ...), condition=%wide.region_4.4_spmd.clone, body=%wide.region_3.3_spmd.clone.sunk | while | flops 271712256 | bytes 9636090 | solution.py:131
  162.0 2.3 mul.350
  166.7 3.9 %fusion.32 = f32[64,1024]{1,0:T(8,128)S(1)} fusion(f32[128,8,8,128]{3,2,1,0:T(8,128)} %bitcast.76, bf16[64,1024]{1,0:T(8,128)(2,1)S(1)} %get-tuple-element.602, f32[64,1024]{1,0:T(8,128)S(1)} %get-tuple-element.585, bf16[2,64,19,1024]{3,1,2,0:T(8,128)(2,1)} %get-tuple-element.601, s32[]{:T(128)S(6)} %select_n.217, s32[]{:T(128)S(6)} %add.434, ...), kind=kOutput, calls=%fused_computation.6.clone.1 | convolution fusion | flops 271712256 | bytes 5113856 | tf_op jit(solution)/shard_map/while/body/eval_jaxpr/while/body/eval_jaxpr/dot_general | solution.py:127
  173.3 2.3 mul.350
  178.0 3.9 %fusion.32 = f32[64,1024]{1,0:T(8,128)S(1)} fusion(f32[128,8,8,128]{3,2,1,0:T(8,128)} %bitcast.76, bf16[64,1024]{1,0:T(8,128)(2,1)S(1)} %get-tuple-element.602, f32[64,1024]{1,0:T(8,128)S(1)} %get-tuple-element.585, bf16[2,64,19,1024]{3,1,2,0:T(8,128)(2,1)} %get-tuple-element.601, s32[]{:T(128)S(6)} %select_n.217, s32[]{:T(128)S(6)} %add.434, ...), kind=kOutput, calls=%fused_computation.6.clone.1 | convolution fusion | flops 271712256 | bytes 5113856 | tf_op jit(solution)/shard_map/while/body/eval_jaxpr/while/body/eval_jaxpr/dot_general | solution.py:127
  184.6 2.3 mul.350
  189.4 3.9 %fusion.32 = f32[64,1024]{1,0:T(8,128)S(1)} fusion(f32[128,8,8,128]{3,2,1,0:T(8,128)} %bitcast.76, bf16[64,1024]{1,0:T(8,128)(2,1)S(1)} %get-tuple-element.602, f32[64,1024]{1,0:T(8,128)S(1)} %get-tuple-element.585, bf16[2,64,19,1024]{3,1,2,0:T(8,128)(2,1)} %get-tuple-element.601, s32[]{:T(128)S(6)} %select_n.217, s32[]{:T(128)S(6)} %add.434, ...), kind=kOutput, calls=%fused_computation.6.clone.1 | convolution fusion | flops 271712256 | bytes 5113856 | tf_op jit(solution)/shard_map/while/body/eval_jaxpr/while/body/eval_jaxpr/dot_general | solution.py:127
  196.0 2.3 mul.350
  200.7 3.9 %fusion.32 = f32[64,1024]{1,0:T(8,128)S(1)} fusion(f32[128,8,8,128]{3,2,1,0:T(8,128)} %bitcast.76, bf16[64,1024]{1,0:T(8,128)(2,1)S(1)} %get-tuple-element.602, f32[64,1024]{1,0:T(8,128)S(1)} %get-tuple-element.585, bf16[2,64,19,1024]{3,1,2,0:T(8,128)(2,1)} %get-tuple-element.601, s32[]{:T(128)S(6)} %select_n.217, s32[]{:T(128)S(6)} %add.434, ...), kind=kOutput, calls=%fused_computation.6.clone.1 | convolution fusion | flops 271712256 | bytes 5113856 | tf_op jit(solution)/shard_map/while/body/eval_jaxpr/while/body/eval_jaxpr/dot_general | solution.py:127
  207.3 2.3 mul.350
  212.0 3.9 %fusion.32 = f32[64,1024]{1,0:T(8,128)S(1)} fusion(f32[128,8,8,128]{3,2,1,0:T(8,128)} %bitcast.76, bf16[64,1024]{1,0:T(8,128)(2,1)S(1)} %get-tuple-element.602, f32[64,1024]{1,0:T(8,128)S(1)} %get-tuple-element.585, bf16[2,64,19,1024]{3,1,2,0:T(8,128)(2,1)} %get-tuple-element.601, s32[]{:T(128)S(6)} %select_n.217, s32[]{:T(128)S(6)} %add.434, ...), kind=kOutput, calls=%fused_computation.6.clone.1 | convolution fusion | flops 271712256 | bytes 5113856 | tf_op jit(solution)/shard_map/while/body/eval_jaxpr/while/body/eval_jaxpr/dot_general | solution.py:127
  218.6 2.3 mul.350
  223.4 3.9 %fusion.32 = f32[64,1024]{1,0:T(8,128)S(1)} fusion(f32[128,8,8,128]{3,2,1,0:T(8,128)} %bitcast.76, bf16[64,1024]{1,0:T(8,128)(2,1)S(1)} %get-tuple-element.602, f32[64,1024]{1,0:T(8,128)S(1)} %get-tuple-element.585, bf16[2,64,19,1024]{3,1,2,0:T(8,128)(2,1)} %get-tuple-element.601, s32[]{:T(128)S(6)} %select_n.217, s32[]{:T(128)S(6)} %add.434, ...), kind=kOutput, calls=%fused_computation.6.clone.1 | convolution fusion | flops 271712256 | bytes 5113856 | tf_op jit(solution)/shard_map/while/body/eval_jaxpr/while/body/eval_jaxpr/dot_general | solution.py:127
  230.0 2.3 mul.350
  234.7 3.9 %fusion.32 = f32[64,1024]{1,0:T(8,128)S(1)} fusion(f32[128,8,8,128]{3,2,1,0:T(8,128)} %bitcast.76, bf16[64,1024]{1,0:T(8,128)(2,1)S(1)} %get-tuple-element.602, f32[64,1024]{1,0:T(8,128)S(1)} %get-tuple-element.585, bf16[2,64,19,1024]{3,1,2,0:T(8,128)(2,1)} %get-tuple-element.601, s32[]{:T(128)S(6)} %select_n.217, s32[]{:T(128)S(6)} %add.434, ...), kind=kOutput, calls=%fused_computation.6.clone.1 | convolution fusion | flops 271712256 | bytes 5113856 | tf_op jit(solution)/shard_map/while/body/eval_jaxpr/while/body/eval_jaxpr/dot_general | solution.py:127
  241.3 2.3 mul.350
  246.0 3.9 %fusion.32 = f32[64,1024]{1,0:T(8,128)S(1)} fusion(f32[128,8,8,128]{3,2,1,0:T(8,128)} %bitcast.76, bf16[64,1024]{1,0:T(8,128)(2,1)S(1)} %get-tuple-element.602, f32[64,1024]{1,0:T(8,128)S(1)} %get-tuple-element.585, bf16[2,64,19,1024]{3,1,2,0:T(8,128)(2,1)} %get-tuple-element.601, s32[]{:T(128)S(6)} %select_n.217, s32[]{:T(128)S(6)} %add.434, ...), kind=kOutput, calls=%fused_computation.6.clone.1 | convolution fusion | flops 271712256 | bytes 5113856 | tf_op jit(solution)/shard_map/while/body/eval_jaxpr/while/body/eval_jaxpr/dot_general | solution.py:127
  252.6 2.3 mul.350
  257.4 3.9 %fusion.32 = f32[64,1024]{1,0:T(8,128)S(1)} fusion(f32[128,8,8,128]{3,2,1,0:T(8,128)} %bitcast.76, bf16[64,1024]{1,0:T(8,128)(2,1)S(1)} %get-tuple-element.602, f32[64,1024]{1,0:T(8,128)S(1)} %get-tuple-element.585, bf16[2,64,19,1024]{3,1,2,0:T(8,128)(2,1)} %get-tuple-element.601, s32[]{:T(128)S(6)} %select_n.217, s32[]{:T(128)S(6)} %add.434, ...), kind=kOutput, calls=%fused_computation.6.clone.1 | convolution fusion | flops 271712256 | bytes 5113856 | tf_op jit(solution)/shard_map/while/body/eval_jaxpr/while/body/eval_jaxpr/dot_general | solution.py:127
  262.2 101.9 %while.44 = (s32[]{:T(128)}, f32[64,1024]{1,0:T(8,128)S(1)}, s32[2,9]{1,0:T(2,128)S(1)}, s32[]{:T(128)}, bf16[2,64,19,1024]{3,1,2,0:T(8,128)(2,1)}, /*index=5*/b...) while((s32[]{:T(128)}, f32[64,1024]{1,0:T(8,128)S(1)}, ...), condition=%wide.region_4.4_spmd.clone, body=%wide.region_3.3_spmd.clone.sunk | while | flops 271712256 | bytes 9636090 | solution.py:131
  264.9 2.3 mul.350
  269.6 3.9 %fusion.32 = f32[64,1024]{1,0:T(8,128)S(1)} fusion(f32[128,8,8,128]{3,2,1,0:T(8,128)} %bitcast.76, bf16[64,1024]{1,0:T(8,128)(2,1)S(1)} %get-tuple-element.602, f32[64,1024]{1,0:T(8,128)S(1)} %get-tuple-element.585, bf16[2,64,19,1024]{3,1,2,0:T(8,128)(2,1)} %get-tuple-element.601, s32[]{:T(128)S(6)} %select_n.217, s32[]{:T(128)S(6)} %add.434, ...), kind=kOutput, calls=%fused_computation.6.clone.1 | convolution fusion | flops 271712256 | bytes 5113856 | tf_op jit(solution)/shard_map/while/body/eval_jaxpr/while/body/eval_jaxpr/dot_general | solution.py:127
  276.2 2.3 mul.350
  281.0 3.9 %fusion.32 = f32[64,1024]{1,0:T(8,128)S(1)} fusion(f32[128,8,8,128]{3,2,1,0:T(8,128)} %bitcast.76, bf16[64,1024]{1,0:T(8,128)(2,1)S(1)} %get-tuple-element.602, f32[64,1024]{1,0:T(8,128)S(1)} %get-tuple-element.585, bf16[2,64,19,1024]{3,1,2,0:T(8,128)(2,1)} %get-tuple-element.601, s32[]{:T(128)S(6)} %select_n.217, s32[]{:T(128)S(6)} %add.434, ...), kind=kOutput, calls=%fused_computation.6.clone.1 | convolution fusion | flops 271712256 | bytes 5113856 | tf_op jit(solution)/shard_map/while/body/eval_jaxpr/while/body/eval_jaxpr/dot_general | solution.py:127
  287.5 2.3 mul.350
  292.3 3.9 %fusion.32 = f32[64,1024]{1,0:T(8,128)S(1)} fusion(f32[128,8,8,128]{3,2,1,0:T(8,128)} %bitcast.76, bf16[64,1024]{1,0:T(8,128)(2,1)S(1)} %get-tuple-element.602, f32[64,1024]{1,0:T(8,128)S(1)} %get-tuple-element.585, bf16[2,64,19,1024]{3,1,2,0:T(8,128)(2,1)} %get-tuple-element.601, s32[]{:T(128)S(6)} %select_n.217, s32[]{:T(128)S(6)} %add.434, ...), kind=kOutput, calls=%fused_computation.6.clone.1 | convolution fusion | flops 271712256 | bytes 5113856 | tf_op jit(solution)/shard_map/while/body/eval_jaxpr/while/body/eval_jaxpr/dot_general | solution.py:127
  303.6 3.9 %fusion.32 = f32[64,1024]{1,0:T(8,128)S(1)} fusion(f32[128,8,8,128]{3,2,1,0:T(8,128)} %bitcast.76, bf16[64,1024]{1,0:T(8,128)(2,1)S(1)} %get-tuple-element.602, f32[64,1024]{1,0:T(8,128)S(1)} %get-tuple-element.585, bf16[2,64,19,1024]{3,1,2,0:T(8,128)(2,1)} %get-tuple-element.601, s32[]{:T(128)S(6)} %select_n.217, s32[]{:T(128)S(6)} %add.434, ...), kind=kOutput, calls=%fused_computation.6.clone.1 | convolution fusion | flops 271712256 | bytes 5113856 | tf_op jit(solution)/shard_map/while/body/eval_jaxpr/while/body/eval_jaxpr/dot_general | solution.py:127
  314.9 3.9 %fusion.32 = f32[64,1024]{1,0:T(8,128)S(1)} fusion(f32[128,8,8,128]{3,2,1,0:T(8,128)} %bitcast.76, bf16[64,1024]{1,0:T(8,128)(2,1)S(1)} %get-tuple-element.602, f32[64,1024]{1,0:T(8,128)S(1)} %get-tuple-element.585, bf16[2,64,19,1024]{3,1,2,0:T(8,128)(2,1)} %get-tuple-element.601, s32[]{:T(128)S(6)} %select_n.217, s32[]{:T(128)S(6)} %add.434, ...), kind=kOutput, calls=%fused_computation.6.clone.1 | convolution fusion | flops 271712256 | bytes 5113856 | tf_op jit(solution)/shard_map/while/body/eval_jaxpr/while/body/eval_jaxpr/dot_general | solution.py:127
  326.3 3.9 %fusion.32 = f32[64,1024]{1,0:T(8,128)S(1)} fusion(f32[128,8,8,128]{3,2,1,0:T(8,128)} %bitcast.76, bf16[64,1024]{1,0:T(8,128)(2,1)S(1)} %get-tuple-element.602, f32[64,1024]{1,0:T(8,128)S(1)} %get-tuple-element.585, bf16[2,64,19,1024]{3,1,2,0:T(8,128)(2,1)} %get-tuple-element.601, s32[]{:T(128)S(6)} %select_n.217, s32[]{:T(128)S(6)} %add.434, ...), kind=kOutput, calls=%fused_computation.6.clone.1 | convolution fusion | flops 271712256 | bytes 5113856 | tf_op jit(solution)/shard_map/while/body/eval_jaxpr/while/body/eval_jaxpr/dot_general | solution.py:127
  337.6 3.9 %fusion.32 = f32[64,1024]{1,0:T(8,128)S(1)} fusion(f32[128,8,8,128]{3,2,1,0:T(8,128)} %bitcast.76, bf16[64,1024]{1,0:T(8,128)(2,1)S(1)} %get-tuple-element.602, f32[64,1024]{1,0:T(8,128)S(1)} %get-tuple-element.585, bf16[2,64,19,1024]{3,1,2,0:T(8,128)(2,1)} %get-tuple-element.601, s32[]{:T(128)S(6)} %select_n.217, s32[]{:T(128)S(6)} %add.434, ...), kind=kOutput, calls=%fused_computation.6.clone.1 | convolution fusion | flops 271712256 | bytes 5113856 | tf_op jit(solution)/shard_map/while/body/eval_jaxpr/while/body/eval_jaxpr/dot_general | solution.py:127
  348.9 3.9 %fusion.32 = f32[64,1024]{1,0:T(8,128)S(1)} fusion(f32[128,8,8,128]{3,2,1,0:T(8,128)} %bitcast.76, bf16[64,1024]{1,0:T(8,128)(2,1)S(1)} %get-tuple-element.602, f32[64,1024]{1,0:T(8,128)S(1)} %get-tuple-element.585, bf16[2,64,19,1024]{3,1,2,0:T(8,128)(2,1)} %get-tuple-element.601, s32[]{:T(128)S(6)} %select_n.217, s32[]{:T(128)S(6)} %add.434, ...), kind=kOutput, calls=%fused_computation.6.clone.1 | convolution fusion | flops 271712256 | bytes 5113856 | tf_op jit(solution)/shard_map/while/body/eval_jaxpr/while/body/eval_jaxpr/dot_general | solution.py:127
  360.2 3.9 %fusion.32 = f32[64,1024]{1,0:T(8,128)S(1)} fusion(f32[128,8,8,128]{3,2,1,0:T(8,128)} %bitcast.76, bf16[64,1024]{1,0:T(8,128)(2,1)S(1)} %get-tuple-element.602, f32[64,1024]{1,0:T(8,128)S(1)} %get-tuple-element.585, bf16[2,64,19,1024]{3,1,2,0:T(8,128)(2,1)} %get-tuple-element.601, s32[]{:T(128)S(6)} %select_n.217, s32[]{:T(128)S(6)} %add.434, ...), kind=kOutput, calls=%fused_computation.6.clone.1 | convolution fusion | flops 271712256 | bytes 5113856 | tf_op jit(solution)/shard_map/while/body/eval_jaxpr/while/body/eval_jaxpr/dot_general | solution.py:127
  364.5 20.2 %all_to_all.45 = bf16[64,2,1024]{2,1,0:T(2,128)(2,1)S(1)} all-to-all(bf16[64,2,1024]{2,1,0:T(2,128)(2,1)S(1)} %copy.51), channel_id=1, replica_groups=mesh['tile'=16,'mem'=16] {'mem'}, dimensions={0} | all-to-all | bytes 524288 | tf_op jit(solution)/shard_map/all_to_all | solution.py:144
  (148 shorter events, 57.7 us)
Async XLA Ops:
  0.0 46.6 %copy-start = (s32[9]{0:T(128)S(1)}, s32[9]{0:T(128)}, u32[]{:S(2)}) copy-start(s32[9]{0:T(128)} %constant.262.clone) | copy-start | bytes 112
  0.0 53.2 %copy-start.4 = (s32[2,9]{1,0:T(2,128)S(1)}, s32[2,9]{1,0:T(2,128)}, u32[]{:S(2)}) copy-start(s32[2,9]{1,0:T(2,128)} %param.14) | copy-start | bytes 220
  1.9 20.9 %all-to-all-start.1 = ((bf16[4,32,1024]{2,0,1:T(4,128)(2,1)}), bf16[4,32,1024]{2,0,1:T(4,128)(2,1)S(1)}, u32[]{:S(2)}, u32[]{:S(2)}) async-start(bf16[4,32,1024]{2,0,1:T(4,128)(2,1)} %copy.49), calls=%async_computation.1 | async-start | bytes 524288 | tf_op jit(solution)/shard_map/all_to_all | solution.py:75
  22.7 20.2 %all-to-all-start = ((f32[4,32,1024]{2,0,1:T(4,128)}), f32[4,32,1024]{2,0,1:T(4,128)S(1)}, u32[]{:S(2)}, u32[]{:S(2)}) async-start(f32[4,32,1024]{2,0,1:T(4,128)} %copy.42), calls=%async_computation | async-start | bytes 1048576 | tf_op jit(solution)/shard_map/all_to_all | solution.py:72
  43.5 33.4 %collective-permute-start = (bf16[2,64,2,1024]{3,1,2,0:T(8,128)(2,1)S(1)}, bf16[2,64,2,1024]{3,1,2,0:T(8,128)(2,1)}, u32[]{:S(2)}, u32[]{:S(2)}) collective-permute-start(bf16[2,64,2,1024]{3,1,2,0:T(8,128)(2,1)S(1)} %pad_maximum_fusion), channel_id=1, source_target_pairs={{0,5},{1,6},{2,7},{3,8},{4,9},{5,10},{6,11},{7,12},{8,13},{9,14},{... | collective-permute-start | bytes 1572872 | tf_op jit(solution)/shard_map/ppermute | solution.py:17
  47.4 41.7 %collective-permute-start.1 = (bf16[2,64,2,1024]{3,1,2,0:T(8,128)(2,1)S(1)}, bf16[2,64,2,1024]{3,1,2,0:T(8,128)(2,1)}, u32[]{:S(2)}, u32[]{:S(2)}) collective-permute-start(bf16[2,64,2,1024]{3,1,2,0:T(8,128)(2,1)S(1)} %pad_maximum_fusion), channel_id=1, source_target_pairs={{0,4},{1,5},{2,6},{3,7},{4,8},{5,9},{6,10},{7,11},{8,12},{9,13},{1... | collective-permute-start | bytes 1572872 | tf_op jit(solution)/shard_map/ppermute | solution.py:17
  50.5 64.9 %collective-permute-start.2 = (bf16[2,64,2,1024]{3,1,2,0:T(8,128)(2,1)S(1)}, bf16[2,64,2,1024]{3,1,2,0:T(8,128)(2,1)S(1)}, u32[]{:S(2)}, u32[]{:S(2)}) collective-permute-start(bf16[2,64,2,1024]{3,1,2,0:T(8,128)(2,1)S(1)} %pad_maximum_fusion), channel_id=1, source_target_pairs={{0,3},{1,4},{2,5},{3,6},{4,7},{5,8},{6,9},{7,10},{8,11},{9,12},{10... | collective-permute-start | bytes 1572872 | tf_op jit(solution)/shard_map/ppermute | solution.py:17
  53.4 64.9 %collective-permute-start.3 = (bf16[2,64,2,1024]{3,1,2,0:T(8,128)(2,1)S(1)}, bf16[2,64,2,1024]{3,1,2,0:T(8,128)(2,1)S(1)}, u32[]{:S(2)}, u32[]{:S(2)}) collective-permute-start(bf16[2,64,2,1024]{3,1,2,0:T(8,128)(2,1)S(1)} %pad_maximum_fusion), channel_id=1, source_target_pairs={{0,1},{1,2},{2,3},{3,4},{4,5},{5,6},{6,7},{7,8},{8,9},{9,10},{10,1... | collective-permute-start | bytes 1572872 | tf_op jit(solution)/shard_map/ppermute | solution.py:17
  55.4 63.1 %collective-permute-start.4 = (bf16[2,64,2,1024]{3,1,2,0:T(8,128)(2,1)S(1)}, bf16[2,64,2,1024]{3,1,2,0:T(8,128)(2,1)S(1)}, u32[]{:S(2)}, u32[]{:S(2)}) collective-permute-start(bf16[2,64,2,1024]{3,1,2,0:T(8,128)(2,1)S(1)} %pad_maximum_fusion), channel_id=1, source_target_pairs={{1,0},{2,1},{3,2},{4,3},{5,4},{6,5},{7,6},{8,7},{9,8},{10,9},{11,1... | collective-permute-start | bytes 1572872 | tf_op jit(solution)/shard_map/ppermute | solution.py:17
  57.9 100.6 %copy-start.3 = (s32[2,9]{1,0:T(2,128)S(1)}, s32[2,9]{1,0:T(2,128)}, u32[]{:S(2)}) copy-start(s32[2,9]{1,0:T(2,128)} %param.15) | copy-start | bytes 220
  76.9 41.6 %collective-permute-start.5 = (bf16[2,64,2,1024]{3,1,2,0:T(8,128)(2,1)S(1)}, bf16[2,64,2,1024]{3,1,2,0:T(8,128)(2,1)S(1)}, u32[]{:S(2)}, u32[]{:S(2)}) collective-permute-start(bf16[2,64,2,1024]{3,1,2,0:T(8,128)(2,1)S(1)} %pad_maximum_fusion), channel_id=1, source_target_pairs={{3,0},{4,1},{5,2},{6,3},{7,4},{8,5},{9,6},{10,7},{11,8},{12,9},{13... | collective-permute-start | bytes 1572872 | tf_op jit(solution)/shard_map/ppermute | solution.py:17
  89.0 29.5 %collective-permute-start.6 = (bf16[2,64,2,1024]{3,1,2,0:T(8,128)(2,1)S(1)}, bf16[2,64,2,1024]{3,1,2,0:T(8,128)(2,1)S(1)}, u32[]{:S(2)}, u32[]{:S(2)}) collective-permute-start(bf16[2,64,2,1024]{3,1,2,0:T(8,128)(2,1)S(1)} %pad_maximum_fusion), channel_id=1, source_target_pairs={{4,0},{5,1},{6,2},{7,3},{8,4},{9,5},{10,6},{11,7},{12,8},{13,9},{1... | collective-permute-start | bytes 1572872 | tf_op jit(solution)/shard_map/ppermute | solution.py:17
  115.5 40.7 %collective-permute-start.7 = (bf16[2,64,2,1024]{3,1,2,0:T(8,128)(2,1)S(1)}, bf16[2,64,2,1024]{3,1,2,0:T(8,128)(2,1)S(1)}, u32[]{:S(2)}, u32[]{:S(2)}) collective-permute-start(bf16[2,64,2,1024]{3,1,2,0:T(8,128)(2,1)S(1)} %pad_maximum_fusion), channel_id=1, source_target_pairs={{5,0},{6,1},{7,2},{8,3},{9,4},{10,5},{11,6},{12,7},{13,8},{14,9},{... | collective-permute-start | bytes 1572872 | tf_op jit(solution)/shard_map/ppermute | solution.py:17
  156.2 2.2 copy-start.1
  158.4 226.9 %copy-start.2 = (f32[4,32,1024]{2,1,0:T(8,128)S(1)}, f32[4,32,1024]{2,1,0:T(8,128)}, u32[]{:S(2)}) copy-start(f32[4,32,1024]{2,1,0:T(8,128)} %param.11) | copy-start | bytes 1572868
where the time goes:
time: 388 us; the launch traced here: 386 us
  waiting for transfers between devices  111 us (29%)
  local copies, waits for them, and re-layouts  75.6 us (19%)
  matrix products  70.6 us (18%)
  loops' own time  68.7 us (18%)
  starting transfers between devices  33.4 us (9%)
  blocking collectives  20.2 us (5%)
  other arithmetic  5.7 us (1%)
    ppermute x8, waiting for transfers between devices, shifted(): return lax.ppermute(array, axis, pairs)  88.2 us
    dot_general x18, matrix products, add_slot(): lax.dot_general(far_block[1], tapered, (((1,), (1,)), ((), ())), preferre...  70.6 us
    another operation x2, loops' own time, update_block(): lax.fori_loop(0, NB, add_slot, jnp.zeros((every_trial_index, patch_line_l...  68.6 us
    mul x54, local copies, waits for them, and re-layouts, add_slot(): covariance.reshape(VARS, BCELL, VARS, BCELL) * weights[None, :, None, :]  43 us
    ppermute x8, starting transfers between devices, shifted(): return lax.ppermute(array, axis, pairs)  20.8 us
    all_to_all x1, blocking collectives, local(): lax.all_to_all(correction_vectors, 'mem', split_axis=0, concat_axis=1, ti...  20.2 us
    all_to_all x1, waiting for transfers between devices, local(): lax.all_to_all(background_draws, 'mem', split_axis=1, concat_axis=0, tile...  16.4 us
    dynamic_slice x18, local copies, waits for them, and re-layouts, add_slot(): taper_kind = position_kinds[block_index, slot_index]  11 us
  transfers between devices with their start and end apart: 10, of which 6 were waited for; matrix products, arithmetic and copies ran while one was open for 2% of the time, Pallas kernels for 0%

commit v1 on v0

v1 whole, which is shorter than its diff:
```python
import functools

import jax
import jax.numpy as jnp
import ml_dtypes
import numpy as np
from jax import lax
from jax.experimental import pallas as pl
from jax.experimental.pallas import tpu as pltpu
from jax.sharding import PartitionSpec as P

MESH = pl.DeviceIdType.MESH
F32 = jnp.float32
BF16 = jnp.bfloat16
W = 8
GROUPS = 16
NEAR = [1, 15, 2, 14, 3, 13, 4, 12, 5, 11, 6, 10, 7, 9, 8]


def taper_value(dy, dx):
    dy = np.asarray(dy, np.float32)
    dx = np.asarray(dx, np.float32)
    z = np.sqrt(dx * dx + dy * dy) / np.float32(2)
    near = (((np.float32(-0.25) * z + np.float32(0.5)) * z + np.float32(0.625)) * z - np.float32(5 / 3)) * z * z + 1
    safe = np.maximum(z, np.float32(1))
    far = (
        ((((z / np.float32(12) - np.float32(0.5)) * z + np.float32(0.625)) * z + np.float32(5 / 3)) * z - 5) * z
        + 4
        - np.float32(2) / (3 * safe)
    )
    return np.where(z <= 1, near, np.where(z < 2, far, 0)).astype(np.float32)


def side_slots():
    tiles = [[], [], []]
    for row in range(16):
        for depth in (1, 2, 3):
            tile = 0 if row < 5 else 2 if row > 10 else 1
            if row == 5 and depth == 3:
                tile = 0
            if row == 10 and depth == 3:
                tile = 2
            tiles[tile] += [(row, depth, w) for w in range(W)]
    return tiles


def vert_slots():
    return [(row, col, w) for w in range(W) for row in range(3) for col in range(16)]


def corner_slots():
    return [(a, b, w) for a in (1, 2, 3) for b in (1, 2, 3) if (a, b) != (3, 3) for w in range(W)]


def tables():
    sides, vert, corner = side_slots(), vert_slots(), corner_slots()
    select = np.zeros((2, 1024, 1408), np.float32)

    def put(lane, part, row, col, w):
        block, in_row = divmod(row, 8)
        if part is None or block == part:
            select[block, w * 128 + in_row * 16 + col, lane] = 1

    for lane, (row, col, w) in enumerate(vert):
        put(lane, 0, row, col, w)
        put(384 + lane, 0, 5 + row, col, w)
        put(lane, 1, 13 + row, col, w)
        put(384 + lane, 1, 8 + row, col, w)
    for tile in range(3):
        for lane, (row, depth, w) in enumerate(sides[tile]):
            block = row // 8
            at = 768 + (tile - block) * 128 + lane
            put(at, block, row, depth - 1, w)
            put(at + 256, block, row, 16 - depth, w)
    for lane, (a, b, w) in enumerate(corner):
        put(1280 + lane, 0, a - 1, 16 - b, w)
        put(1344 + lane, 0, a - 1, b - 1, w)
        put(1280 + lane, 1, 16 - a, 16 - b, w)
        put(1344 + lane, 1, 16 - a, b - 1, w)

    weights = np.zeros((4, 64, 1024), np.float32)
    kinds = np.full((4, 1024), 4, np.int32)
    self_weights = np.zeros((2, 64, 128), np.float32)
    cell = np.arange(64)
    for s in range(4):
        block = s // 2
        own_row, own_col = 4 * s + cell // 16, cell % 16
        slots = [None] * 1024
        base = [-3, 8, 5, 16][s]
        for lane, (row, col, w) in enumerate(vert):
            slots[lane] = (base + row, col)
        if s in (0, 3):
            for lane, (a, b, w) in enumerate(corner):
                row = -a if s == 0 else 15 + a
                slots[384 + lane] = (row, -b)
                slots[448 + lane] = (row, 15 + b)
        for k in range(2):
            for lane, (row, depth, w) in enumerate(sides[k + (s >= 2)]):
                slots[512 + 128 * k + lane] = (row, -depth)
                slots[768 + 128 * k + lane] = (row, 15 + depth)
        for lane, slot in enumerate(slots):
            if slot is not None:
                row, col = slot
                weights[s, :, lane] = taper_value(row - own_row, col - own_col) / np.float32(63)
                kinds[s, lane] = 3 * (row // 8 - block + 1) + col // 16 + 1
        if s < 2:
            every = np.arange(128)
            self_weights[s] = taper_value(
                (every // 16)[None] - own_row[:, None], (every % 16)[None] - own_col[:, None]
            ) / np.float32(63)
    return select.astype(ml_dtypes.bfloat16), weights, kinds, self_weights


UP, DN, TL, TR, CU, CD = 0, 384, 768, 1152, 1536, 1664
VUP, VDN, LEFT, RIGHT, CUL, CUR, CDL, CDR = 0, 384, 768, 1152, 1536, 1664, 1792, 1920


def kernel(
    bg_ref, inn_ref, tally_ref, kinds_ref, region_ref, selfw_ref, sel_hbm, weight_hbm,
    out_ref,
    sel, weight, mask_out, mask_in, ha, hl, hi, stage, ca, ci, ra, ri, fa, fi, xa, xi, at, hsa, hsi, rha, rhi,
    inner, exta, exti, tt, acc, rs, cb, rb, fb,
    const_sem, mask_send, mask_recv, as_, ar_, is_, ir_, hs_, hr_, gs_, gr_, bs_, br_,
):
    t = lax.axis_index("tile")
    me = lax.axis_index("mem")
    z, c = me // 2, me % 2
    left, right = 2 * ((z + 7) % 8), 2 * ((z + 1) % 8)
    up_tile, down_tile = (t + 15 + c) % 16, (t + c) % 16
    other = 1 - c

    across = (t + 15 + 2 * c) % 16
    barrier = pltpu.get_barrier_semaphore()
    for k in range(1, GROUPS):
        pl.semaphore_signal(barrier, inc=1, device_id=(t, (me + k) % GROUPS), device_id_type=MESH)
    for base in (left, 2 * z, right):
        pl.semaphore_signal(barrier, inc=1, device_id=(across, base + other), device_id_type=MESH)

    load_sel = pltpu.make_async_copy(sel_hbm, sel, const_sem.at[0])
    load_weight = pltpu.make_async_copy(weight_hbm, weight, const_sem.at[1])
    load_sel.start()
    load_weight.start()

    lane8 = lax.broadcasted_iota(jnp.int32, (8, 128), 1)
    for q in range(2):
        held = jnp.where(lane8 == 4, 1.0, 0.0)
        for s in range(9):
            held = jnp.where(kinds_ref[q : q + 1, s : s + 1] == lane8, 1.0, held)
        mask_out[q] = held

    for r in range(4):
        rows = slice(8 * r, 8 * r + 8)
        for w in range(W):
            lanes = slice(128 * w, 128 * w + 128)
            x0, x1, x2, x3 = (bg_ref[m, rows, lanes] for m in range(4))
            s01, d01, s23, d23 = x0 + x1, x0 - x1, x2 + x3, x2 - x3
            h0 = (s01 + s23) * 0.5
            high = h0.astype(BF16).astype(F32)
            base = (r // 2) * 64 + (r % 2) * 8
            ha[w, base : base + 8, :] = high
            ha[w, base + 16 : base + 24, :] = (s01 - s23) * 0.5
            ha[w, base + 32 : base + 40, :] = (d01 + d23) * 0.5
            ha[w, base + 48 : base + 56, :] = (d01 - d23) * 0.5
            hl[w, rows, :] = h0 - high
    for w in range(W):
        for m in range(4):
            y = inn_ref[m, :, 128 * w : 128 * w + 128].astype(F32)
            for r in range(4):
                base = (r // 2) * 64 + m * 16 + (r % 2) * 8
                hi[w, base : base + 8, :] = y[8 * r : 8 * r + 8, :]

    def build(dest, carry):
        col, core = dest // 2, dest % 2
        for w in range(0, W, 2):
            for source, chunk in ((ha, ca), (hi, ci)):
                a = source[w, pl.ds(core * 64 + col, 8, stride=8), :]
                b = source[w + 1, pl.ds(core * 64 + col, 8, stride=8), :]
                chunk[dest, 8 * w : 8 * w + 16, :] = jnp.concatenate([a, b], axis=0).astype(BF16)
        for w in range(W):
            stage[2 * w : 2 * w + 2, :] = hl[w, pl.ds(core * 16 + col, 2, stride=8), :]
        ca[dest, 64:80, :] = stage[...].astype(BF16)
        return carry

    lax.fori_loop(0, GROUPS, build, 0)

    pl.semaphore_wait(barrier, GROUPS + 2)

    mask_row = me // 4

    def mask_copy(q):
        target = 2 * (2 * (me % 4) + q) + mask_row // 2
        return target, pltpu.make_async_remote_copy(
            src_ref=mask_out.at[q], dst_ref=mask_in.at[mask_row % 2], send_sem=mask_send.at[q],
            recv_sem=mask_recv.at[mask_row % 2], device_id=(t, target), device_id_type=MESH,
        )

    for q in range(2):
        target, copy = mask_copy(q)

        @pl.when(target != me)
        def _(copy=copy):
            copy.start()

        @pl.when(target == me)
        def _(q=q):
            mask_in[mask_row % 2] = mask_out[q]

    def spread(source, landing, send, recv):
        copies = {}
        for k in NEAR:
            peer = (me + k) % GROUPS
            copies[k] = pltpu.make_async_remote_copy(
                src_ref=source.at[peer], dst_ref=landing.at[me], send_sem=send.at[k], recv_sem=recv.at[k],
                device_id=(t, peer), device_id_type=MESH,
            )
            copies[k].start()
        return copies

    a_copies = spread(ca, ra, as_, ar_)
    i_copies = spread(ci, ri, is_, ir_)

    load_sel.wait()
    load_weight.wait()
    for b in range(2):
        @pl.when(4 * (2 * c + b) + z // 2 != me)
        def _(b=b):
            pltpu.make_async_remote_copy(
                src_ref=mask_out.at[0], dst_ref=mask_in.at[b], send_sem=mask_send.at[0], recv_sem=mask_recv.at[b],
                device_id=(t, (me + 1) % GROUPS), device_id_type=MESH,
            ).wait_recv()

    for s in range(4):
        block = s // 2
        region = region_ref[s : s + 1, :]
        row = jnp.zeros((1, 1024), F32)
        for k in ((0, 1, 2, 3, 5), (3, 5, 6, 7, 8), (0, 1, 2, 3, 5), (3, 5, 6, 7, 8))[s]:
            row = jnp.where(region == k, mask_in[block, 0:1, k : k + 1], row)
        weight[s] = weight[s] * row

    def halo(hs, rh, send, recv):
        plan = [
            (UP, VDN, 384, (up_tile, 2 * z + other), 1),
            (DN, VUP, 384, (down_tile, 2 * z + other), 0),
            (TL, RIGHT, 384, (t, left + c), 3),
            (TR, LEFT, 384, (t, right + c), 2),
            (CU, CDL, 128, (up_tile, right + other), 6),
            (CU, CDR, 128, (up_tile, left + other), 7),
            (CD, CUL, 128, (down_tile, right + other), 4),
            (CD, CUR, 128, (down_tile, left + other), 5),
        ]
        copies = []
        for source, landing, width, device, n in plan:
            copy = pltpu.make_async_remote_copy(
                src_ref=hs.at[:, source : source + width], dst_ref=rh.at[:, landing : landing + width],
                send_sem=send.at[n], recv_sem=recv.at[n], device_id=device, device_id_type=MESH,
            )
            copy.start()
            copies.append(copy)
        return copies

    def pick(x, hs, inner_at):
        m0 = jnp.dot(x[0], sel[0], preferred_element_type=F32)
        m1 = jnp.dot(x[1], sel[1], preferred_element_type=F32)
        hs[:, UP : UP + 384] = m0[:, 0:384].astype(BF16)
        hs[:, DN : DN + 384] = m1[:, 0:384].astype(BF16)
        for k, place in enumerate((TL, TR)):
            at0 = 768 + 256 * k
            hs[:, place : place + 128] = m0[:, at0 : at0 + 128].astype(BF16)
            hs[:, place + 128 : place + 256] = (m0[:, at0 + 128 : at0 + 256] + m1[:, at0 : at0 + 128]).astype(BF16)
            hs[:, place + 256 : place + 384] = m1[:, at0 + 128 : at0 + 256].astype(BF16)
        hs[:, CU : CU + 128] = m0[:, 1280:1408].astype(BF16)
        hs[:, CD : CD + 128] = m1[:, 1280:1408].astype(BF16)
        inner[inner_at, 0] = m1[:, 384:768].astype(BF16)
        inner[inner_at, 1] = m0[:, 384:768].astype(BF16)

    def assemble(rh, ext, inner_at):
        first = lax.broadcasted_iota(jnp.int32, (64, 128), 1) < 64
        verts = (rh[:, VUP : VUP + 384], inner[inner_at, 0], inner[inner_at, 1], rh[:, VDN : VDN + 384])
        above = jnp.where(first, rh[:, CUL : CUL + 128].astype(F32), rh[:, CUR : CUR + 128].astype(F32)).astype(BF16)
        below = jnp.where(first, rh[:, CDL : CDL + 128].astype(F32), rh[:, CDR : CDR + 128].astype(F32)).astype(BF16)
        for s in range(4):
            shift = 128 * (s // 2)
            ext[s, :, 0:384] = verts[s]
            ext[s, :, 384:512] = above if s < 2 else below
            ext[s, :, 512:768] = rh[:, LEFT + shift : LEFT + shift + 256]
            ext[s, :, 768:1024] = rh[:, RIGHT + shift : RIGHT + shift + 256]

    fa[pl.ds(pl.multiple_of(me * 80, 8), 80), :] = ca[me].astype(F32)
    for k in NEAR:
        a_copies[k].wait_recv()
        g = (me + GROUPS - k) % GROUPS
        fa[pl.ds(pl.multiple_of(g * 80, 8), 80), :] = ra[g].astype(F32)
    cell = lax.broadcasted_iota(jnp.int32, (1, 128), 1)
    for b in range(2):
        land = jnp.where((8 * (2 * c + b) + z) * 128 + cell < tally_ref[0], 1.0, 0.0)
        for w in range(W):
            lanes = slice(128 * w, 128 * w + 128)
            h0 = fa[pl.ds(8 * w + b, 16, stride=80), :] + fa[pl.ds(64 + 2 * w + b, 16, stride=80), :]
            parts = [h0 - jnp.sum(h0, axis=0, keepdims=True) * (1.0 / GROUPS)]
            parts += [fa[pl.ds(8 * w + 2 * m + b, 16, stride=80), :] for m in (1, 2, 3)]
            tile = jnp.concatenate(parts, axis=0) * land
            xa[b, :, lanes] = tile.astype(BF16)
            turned = tile.T.astype(BF16)
            at[2 * b, 64 * w : 64 * w + 64, :] = turned[0:64]
            at[2 * b + 1, 64 * w : 64 * w + 64, :] = turned[64:128]
    pick(xa, hsa, 0)
    ha_copies = halo(hsa, rha, hs_, hr_)

    def own_taper(s, carry):
        rows = at[s]
        table = selfw_ref[s % 2]
        for n in range(4):
            cov = jnp.dot(rows, xa[s // 2, :, 256 * n : 256 * n + 256], preferred_element_type=F32)
            for h in range(2):
                part = cov[:, 128 * h : 128 * h + 128].reshape(W, 64, 128) * table[None]
                lanes = slice(256 * n + 128 * h, 256 * n + 128 * h + 128)
                tt[s, 0, :, lanes] = part.reshape(512, 128).astype(BF16)
        return carry

    lax.fori_loop(0, 4, own_taper, 0)
    for copy in ha_copies:
        copy.wait_recv()
    assemble(rha, exta, 0)

    def halo_taper(s, carry):
        rows = at[s]
        for n in range(4):
            lanes = slice(256 * n, 256 * n + 256)
            cov = jnp.dot(rows, exta[s, :, lanes], preferred_element_type=F32)
            part = cov.reshape(W, 64, 256) * weight[s, :, lanes][None]
            tt[s, 1, :, lanes] = part.reshape(512, 256).astype(BF16)
        return carry

    lax.fori_loop(0, 4, halo_taper, 0)

    fi[pl.ds(pl.multiple_of(me * 64, 8), 64), :] = ci[me].astype(F32)
    for k in NEAR:
        i_copies[k].wait_recv()
        g = (me + GROUPS - k) % GROUPS
        fi[pl.ds(pl.multiple_of(g * 64, 8), 64), :] = ri[g].astype(F32)
    for b in range(2):
        for w in range(W):
            parts = [fi[pl.ds(8 * w + 2 * m + b, 16, stride=64), :] for m in range(4)]
            xi[b, :, 128 * w : 128 * w + 128] = jnp.concatenate(parts, axis=0).astype(BF16)
    pick(xi, hsi, 1)
    hi_copies = halo(hsi, rhi, gs_, gr_)

    contract = (((1,), (1,)), ((), ()))

    def own_update(s, carry):
        acc[s] = lax.dot_general(tt[s, 0], xi[s // 2], contract, preferred_element_type=F32)
        return carry

    lax.fori_loop(0, 4, own_update, 0)
    for copy in hi_copies:
        copy.wait_recv()
    assemble(rhi, exti, 1)

    def halo_update(s, carry):
        acc[s] = acc[s] + lax.dot_general(tt[s, 1], exti[s], contract, preferred_element_type=F32)
        return carry

    back = {}
    for b in range(2):
        lax.fori_loop(2 * b, 2 * b + 2, halo_update, 0)
        for w in range(W):
            rows = slice(64 * w, 64 * w + 64)
            tile = jnp.concatenate([acc[2 * b, rows, :], acc[2 * b + 1, rows, :]], axis=0).T
            at0 = (8 * b + w) * 64
            rs[at0 : at0 + 64, :] = tile

        def chunk(g, carry, b=b):
            cb[g, b] = rs[pl.ds(512 * b + g, 32, stride=16), :].astype(BF16)
            return carry

        lax.fori_loop(0, GROUPS, chunk, 0)
        for k in NEAR:
            peer = (me + k) % GROUPS
            back[b, k] = pltpu.make_async_remote_copy(
                src_ref=cb.at[peer, b], dst_ref=rb.at[me, b], send_sem=bs_.at[b, k], recv_sem=br_.at[b, k],
                device_id=(t, peer), device_id_type=MESH,
            )
            back[b, k].start()

    for b in range(2):
        fb[pl.ds(pl.multiple_of(me * 64 + 32 * b, 8), 32), :] = cb[me, b].astype(F32)
        for k in NEAR:
            back[b, k].wait_recv()
            g = (me + GROUPS - k) % GROUPS
            fb[pl.ds(pl.multiple_of(g * 64 + 32 * b, 8), 32), :] = rb[g, b].astype(F32)
    for m in range(4):
        for r in range(4):
            rows = slice(8 * r, 8 * r + 8)
            for w in range(W):
                lanes = slice(128 * w, 128 * w + 128)
                update = fb[pl.ds((r // 2) * 64 + (r % 2) * 32 + 4 * w + m, 8, stride=128), :]
                out_ref[m, rows, lanes] = bg_ref[m, rows, lanes] + update

    for copies in (a_copies, i_copies, back):
        for copy in copies.values():
            copy.wait_send()
    for copy in ha_copies + hi_copies:
        copy.wait_send()
    for q in range(2):
        target, copy = mask_copy(q)

        @pl.when(target != me)
        def _(copy=copy):
            copy.wait_send()


def local(background_draws, scaled_residuals, soil_site_tallies, adjacent_patches, position_kinds):
    select, weights, kinds, self_weights = tables()
    vmem = pl.BlockSpec(memory_space=pltpu.VMEM)
    anywhere = pl.BlockSpec(memory_space=pl.ANY)
    sems = pltpu.SemaphoreType.DMA
    return pl.pallas_call(
        kernel,
        out_shape=jax.ShapeDtypeStruct(background_draws.shape, F32),
        in_specs=[vmem, vmem, pl.BlockSpec(memory_space=pltpu.SMEM), vmem, vmem, vmem, anywhere, anywhere],
        out_specs=vmem,
        scratch_shapes=[
            pltpu.VMEM((2, 1024, 1408), BF16),
            pltpu.VMEM((4, 64, 1024), F32),
            pltpu.VMEM((2, 8, 128), F32),
            pltpu.VMEM((2, 8, 128), F32),
            pltpu.VMEM((W, 128, 128), F32),
            pltpu.VMEM((W, 32, 128), F32),
            pltpu.VMEM((W, 128, 128), F32),
            pltpu.VMEM((16, 128), F32),
            pltpu.VMEM((GROUPS, 80, 128), BF16),
            pltpu.VMEM((GROUPS, 64, 128), BF16),
            pltpu.VMEM((GROUPS, 80, 128), BF16),
            pltpu.VMEM((GROUPS, 64, 128), BF16),
            pltpu.VMEM((GROUPS * 80, 128), F32),
            pltpu.VMEM((GROUPS * 64, 128), F32),
            pltpu.VMEM((2, 64, 1024), BF16),
            pltpu.VMEM((2, 64, 1024), BF16),
            pltpu.VMEM((4, 512, 64), BF16),
            pltpu.VMEM((64, 1792), BF16),
            pltpu.VMEM((64, 1792), BF16),
            pltpu.VMEM((64, 2048), BF16),
            pltpu.VMEM((64, 2048), BF16),
            pltpu.VMEM((2, 2, 64, 384), BF16),
            pltpu.VMEM((4, 64, 1024), BF16),
            pltpu.VMEM((4, 64, 1024), BF16),
            pltpu.VMEM((4, 2, 512, 1024), BF16),
            pltpu.VMEM((4, 512, 64), F32),
            pltpu.VMEM((1024, 128), F32),
            pltpu.VMEM((GROUPS, 2, 32, 128), BF16),
            pltpu.VMEM((GROUPS, 2, 32, 128), BF16),
            pltpu.VMEM((GROUPS * 64, 128), F32),
            sems((2,)), sems((2,)), sems((2,)),
            sems((GROUPS,)), sems((GROUPS,)), sems((GROUPS,)), sems((GROUPS,)),
            sems((8,)), sems((8,)), sems((8,)), sems((8,)),
            sems((2, GROUPS)), sems((2, GROUPS)),
        ],
        compiler_params=pltpu.CompilerParams(
            collective_id=0, has_side_effects=True, vmem_limit_bytes=56 * 2**20
        ),
    )(
        background_draws, scaled_residuals, soil_site_tallies, position_kinds,
        jnp.asarray(kinds), jnp.asarray(self_weights), jnp.asarray(select), jnp.asarray(weights),
    )


def solution(mesh):
    in_specs = (
        P("mem", "tile", None),
        P("mem", "tile", None),
        P("tile"),
        P(("tile", "mem"), None),
        P(("tile", "mem"), None),
    )
    out_specs = P("mem", "tile", None)
    return jax.shard_map(local, mesh=mesh, in_specs=in_specs, out_specs=out_specs, check_vma=False)
```

time: 388 us -> 53.2 us (0.14)
  the two profiles are of different devices: /device:TPU:31 before, /device:TPU:1 now
where the time goes in v1:
time: 53.2 us; the launch traced here: 53.1 us
  Pallas kernels  50.5 us (95%)
  local copies, waits for them, and re-layouts  1.89 us (4%)
  between operations  0.66 us (1%)
    pallas_call x1, Pallas kernels, local(): pl.pallas_call(kernel, out_shape=jax.ShapeDtypeStruct(background_draws.sh...  50.5 us
    unnamed x1, local copies, waits for them, and re-layouts  1.89 us

profile of v1, /device:TPU:1, one launch (start us, length us, event | category | flops | bytes accessed | tf_op | source)
XLA Modules:
  0.0 53.1 jit_solution(4560642787246779670)
XLA Ops:
  0.7 50.5 %shard_map.82 = f32[4,32,1024]{2,1,0:T(8,128)} custom-call(f32[4,32,1024]{2,1,0:T(8,128)} %bg_ref.1, bf16[4,32,1024]{2,1,0:T(8,128)(2,1)} %inn_ref.1, s32[1]{0:T(128)S(6)} %copy.10.tally_ref, s32[2,9]{1,0:T(2,128)} %kinds_ref.1, s32[4,1024]{1,0:T(4,128)} %constant.8.clone.region_ref, f32[2,64,128]{2,1,0:T(8,128)} %constant.9.clone.selfw_ref, ...), custom_call_target="tpu_custom_call" | custom-call | tf_op jit(solution)/shard_map/pallas_call | solution.py:417
  51.2 1.9 %copy.11 = f32[4,32,1024]{2,1,0:T(8,128)} copy(f32[4,32,1024]{2,1,0:T(8,128)} %shard_map.82) | data formatting | bytes 1048576

commit v2 on v1

--- a/solution.py
+++ b/solution.py
@@ -2,7 +2,6 @@
 
 import jax
 import jax.numpy as jnp
-import ml_dtypes
 import numpy as np
 from jax import lax
 from jax.experimental import pallas as pl
@@ -54,12 +53,12 @@
 
 def tables():
     sides, vert, corner = side_slots(), vert_slots(), corner_slots()
-    select = np.zeros((2, 1024, 1408), np.float32)
+    select = np.full((2, 1408), -1, np.int32)
 
     def put(lane, part, row, col, w):
         block, in_row = divmod(row, 8)
         if part is None or block == part:
-            select[block, w * 128 + in_row * 16 + col, lane] = 1
+            select[block, lane] = w * 128 + in_row * 16 + col
 
     for lane, (row, col, w) in enumerate(vert):
         put(lane, 0, row, col, w)
@@ -108,7 +107,7 @@
             self_weights[s] = taper_value(
                 (every // 16)[None] - own_row[:, None], (every % 16)[None] - own_col[:, None]
             ) / np.float32(63)
-    return select.astype(ml_dtypes.bfloat16), weights, kinds, self_weights
+    return select, weights, kinds, self_weights
 
 
 UP, DN, TL, TR, CU, CD = 0, 384, 768, 1152, 1536, 1664
@@ -116,7 +115,7 @@
 
 
 def kernel(
-    bg_ref, inn_ref, tally_ref, kinds_ref, region_ref, selfw_ref, sel_hbm, weight_hbm,
+    bg_ref, inn_ref, tally_ref, kinds_ref, region_ref, selfw_ref, select_ref, weight_hbm,
     out_ref,
     sel, weight, mask_out, mask_in, ha, hl, hi, stage, ca, ci, ra, ri, fa, fi, xa, xi, at, hsa, hsi, rha, rhi,
     inner, exta, exti, tt, acc, rs, cb, rb, fb,
@@ -136,9 +135,7 @@
     for base in (left, 2 * z, right):
         pl.semaphore_signal(barrier, inc=1, device_id=(across, base + other), device_id_type=MESH)
 
-    load_sel = pltpu.make_async_copy(sel_hbm, sel, const_sem.at[0])
-    load_weight = pltpu.make_async_copy(weight_hbm, weight, const_sem.at[1])
-    load_sel.start()
+    load_weight = pltpu.make_async_copy(weight_hbm, weight, const_sem)
     load_weight.start()
 
     lane8 = lax.broadcasted_iota(jnp.int32, (8, 128), 1)
@@ -205,37 +202,29 @@
         def _(q=q):
             mask_in[mask_row % 2] = mask_out[q]
 
-    def spread(source, landing, send, recv):
+    def spread(source, landing, send, recv, start=0, size=80):
         copies = {}
         for k in NEAR:
             peer = (me + k) % GROUPS
             copies[k] = pltpu.make_async_remote_copy(
-                src_ref=source.at[peer], dst_ref=landing.at[me], send_sem=send.at[k], recv_sem=recv.at[k],
-                device_id=(t, peer), device_id_type=MESH,
+                src_ref=source.at[peer, pl.ds(start, size)], dst_ref=landing.at[me, pl.ds(start, size)],
+                send_sem=send.at[k], recv_sem=recv.at[k], device_id=(t, peer), device_id_type=MESH,
             )
             copies[k].start()
         return copies
 
     a_copies = spread(ca, ra, as_, ar_)
-    i_copies = spread(ci, ri, is_, ir_)
-
-    load_sel.wait()
-    load_weight.wait()
-    for b in range(2):
-        @pl.when(4 * (2 * c + b) + z // 2 != me)
-        def _(b=b):
-            pltpu.make_async_remote_copy(
-                src_ref=mask_out.at[0], dst_ref=mask_in.at[b], send_sem=mask_send.at[0], recv_sem=mask_recv.at[b],
-                device_id=(t, (me + 1) % GROUPS), device_id_type=MESH,
-            ).wait_recv()
-
-    for s in range(4):
-        block = s // 2
-        region = region_ref[s : s + 1, :]
-        row = jnp.zeros((1, 1024), F32)
-        for k in ((0, 1, 2, 3, 5), (3, 5, 6, 7, 8), (0, 1, 2, 3, 5), (3, 5, 6, 7, 8))[s]:
-            row = jnp.where(region == k, mask_in[block, 0:1, k : k + 1], row)
-        weight[s] = weight[s] * row
+    i_copies = spread(ci, ri, is_, ir_, 0, 64)
+
+    for b in range(2):
+        wanted = select_ref[b : b + 1, :]
+
+        def one_hot(k, carry, b=b, wanted=wanted):
+            entry = lax.broadcasted_iota(jnp.int32, (128, 1408), 0) + 128 * k
+            sel[b, pl.ds(pl.multiple_of(128 * k, 128), 128), :] = jnp.where(entry == wanted, 1.0, 0.0).astype(BF16)
+            return carry
+
+        lax.fori_loop(0, 8, one_hot, 0)
 
     def halo(hs, rh, send, recv):
         plan = [
@@ -300,11 +289,43 @@
             parts += [fa[pl.ds(8 * w + 2 * m + b, 16, stride=80), :] for m in (1, 2, 3)]
             tile = jnp.concatenate(parts, axis=0) * land
             xa[b, :, lanes] = tile.astype(BF16)
-            turned = tile.T.astype(BF16)
+    pick(xa, hsa, 0)
+    ha_copies = halo(hsa, rha, hs_, hr_)
+
+    fi[pl.ds(pl.multiple_of(me * 64, 8), 64), :] = ci[me].astype(F32)
+    for k in NEAR:
+        i_copies[k].wait_recv()
+        g = (me + GROUPS - k) % GROUPS
+        fi[pl.ds(pl.multiple_of(g * 64, 8), 64), :] = ri[g].astype(F32)
+    for b in range(2):
+        for w in range(W):
+            parts = [fi[pl.ds(8 * w + 2 * m + b, 16, stride=64), :] for m in range(4)]
+            xi[b, :, 128 * w : 128 * w + 128] = jnp.concatenate(parts, axis=0).astype(BF16)
+    pick(xi, hsi, 1)
+    hi_copies = halo(hsi, rhi, gs_, gr_)
+
+    for b in range(2):
+        for w in range(W):
+            turned = xa[b, :, 128 * w : 128 * w + 128].astype(F32).T.astype(BF16)
             at[2 * b, 64 * w : 64 * w + 64, :] = turned[0:64]
             at[2 * b + 1, 64 * w : 64 * w + 64, :] = turned[64:128]
-    pick(xa, hsa, 0)
-    ha_copies = halo(hsa, rha, hs_, hr_)
+    load_weight.wait()
+    for b in range(2):
+        @pl.when(4 * (2 * c + b) + z // 2 != me)
+        def _(b=b):
+            pltpu.make_async_remote_copy(
+                src_ref=mask_out.at[0], dst_ref=mask_in.at[b], send_sem=mask_send.at[0], recv_sem=mask_recv.at[b],
+                device_id=(t, (me + 1) % GROUPS), device_id_type=MESH,
+            ).wait_recv()
+
+    for s in range(4):
+        block = s // 2
+        region = region_ref[s : s + 1, :]
+        row = jnp.zeros((1, 1024), F32)
+        for k in ((0, 1, 2, 3, 5), (3, 5, 6, 7, 8), (0, 1, 2, 3, 5), (3, 5, 6, 7, 8))[s]:
+            row = jnp.where(region == k, mask_in[block, 0:1, k : k + 1], row)
+        weight[s] = weight[s] * row
+
 
     def own_taper(s, carry):
         rows = at[s]
@@ -318,6 +339,13 @@
         return carry
 
     lax.fori_loop(0, 4, own_taper, 0)
+    contract = (((1,), (1,)), ((), ()))
+
+    def own_update(s, carry):
+        acc[s] = lax.dot_general(tt[s, 0], xi[s // 2], contract, preferred_element_type=F32)
+        return carry
+
+    lax.fori_loop(0, 4, own_update, 0)
     for copy in ha_copies:
         copy.wait_recv()
     assemble(rha, exta, 0)
@@ -333,25 +361,6 @@
 
     lax.fori_loop(0, 4, halo_taper, 0)
 
-    fi[pl.ds(pl.multiple_of(me * 64, 8), 64), :] = ci[me].astype(F32)
-    for k in NEAR:
-        i_copies[k].wait_recv()
-        g = (me + GROUPS - k) % GROUPS
-        fi[pl.ds(pl.multiple_of(g * 64, 8), 64), :] = ri[g].astype(F32)
-    for b in range(2):
-        for w in range(W):
-            parts = [fi[pl.ds(8 * w + 2 * m + b, 16, stride=64), :] for m in range(4)]
-            xi[b, :, 128 * w : 128 * w + 128] = jnp.concatenate(parts, axis=0).astype(BF16)
-    pick(xi, hsi, 1)
-    hi_copies = halo(hsi, rhi, gs_, gr_)
-
-    contract = (((1,), (1,)), ((), ()))
-
-    def own_update(s, carry):
-        acc[s] = lax.dot_general(tt[s, 0], xi[s // 2], contract, preferred_element_type=F32)
-        return carry
-
-    lax.fori_loop(0, 4, own_update, 0)
     for copy in hi_copies:
         copy.wait_recv()
     assemble(rhi, exti, 1)
@@ -389,12 +398,10 @@
             g = (me + GROUPS - k) % GROUPS
             fb[pl.ds(pl.multiple_of(g * 64 + 32 * b, 8), 32), :] = rb[g, b].astype(F32)
     for m in range(4):
-        for r in range(4):
-            rows = slice(8 * r, 8 * r + 8)
+        for core in range(2):
             for w in range(W):
-                lanes = slice(128 * w, 128 * w + 128)
-                update = fb[pl.ds((r // 2) * 64 + (r % 2) * 32 + 4 * w + m, 8, stride=128), :]
-                out_ref[m, rows, lanes] = bg_ref[m, rows, lanes] + update
+                pair = [fb[pl.ds(core * 64 + b * 32 + 4 * w + m, 8, stride=128), :] for b in range(2)]
+                out_ref[m, 16 * core : 16 * core + 16, 128 * w : 128 * w + 128] = jnp.concatenate(pair, axis=0).astype(BF16)
 
     for copies in (a_copies, i_copies, back):
         for copy in copies.values():
@@ -414,10 +421,10 @@
     vmem = pl.BlockSpec(memory_space=pltpu.VMEM)
     anywhere = pl.BlockSpec(memory_space=pl.ANY)
     sems = pltpu.SemaphoreType.DMA
-    return pl.pallas_call(
+    increments = pl.pallas_call(
         kernel,
-        out_shape=jax.ShapeDtypeStruct(background_draws.shape, F32),
-        in_specs=[vmem, vmem, pl.BlockSpec(memory_space=pltpu.SMEM), vmem, vmem, vmem, anywhere, anywhere],
+        out_shape=jax.ShapeDtypeStruct(background_draws.shape, BF16),
+        in_specs=[vmem, vmem, pl.BlockSpec(memory_space=pltpu.SMEM), vmem, vmem, vmem, vmem, anywhere],
         out_specs=vmem,
         scratch_shapes=[
             pltpu.VMEM((2, 1024, 1408), BF16),
@@ -450,7 +457,7 @@
             pltpu.VMEM((GROUPS, 2, 32, 128), BF16),
             pltpu.VMEM((GROUPS, 2, 32, 128), BF16),
             pltpu.VMEM((GROUPS * 64, 128), F32),
-            sems((2,)), sems((2,)), sems((2,)),
+            sems(()), sems((2,)), sems((2,)),
             sems((GROUPS,)), sems((GROUPS,)), sems((GROUPS,)), sems((GROUPS,)),
             sems((8,)), sems((8,)), sems((8,)), sems((8,)),
             sems((2, GROUPS)), sems((2, GROUPS)),
@@ -462,6 +469,7 @@
         background_draws, scaled_residuals, soil_site_tallies, position_kinds,
         jnp.asarray(kinds), jnp.asarray(self_weights), jnp.asarray(select), jnp.asarray(weights),
     )
+    return background_draws + increments.astype(F32)
 
 
 def solution(mesh):

time: 53.2 us -> 48.2 us (0.906)
  Pallas kernels: 50.5 us -> 45.6 us
  local copies, waits for them, and re-layouts: 1.89 us -> 0.01 us
  other arithmetic: 0 us -> 1.8 us
    pallas_call x1, Pallas kernels: 50.5 us -> 45.6 us  [local(): pl.pallas_call(kernel, out_shape=jax.ShapeDtypeStruct(background_draws.sh...]
    unnamed x1 -> x2, local copies, waits for them, and re-layouts: 1.89 us -> 0.01 us
    add x0 -> x1, other arithmetic: none -> 1.8 us  [local(): return background_draws + increments.astype(F32)]
where the time goes in v2:
time: 48.2 us; the launch traced here: 48.1 us
  Pallas kernels  45.6 us (95%)
  other arithmetic  1.8 us (4%)
  between operations  0.68 us (1%)
    pallas_call x1, Pallas kernels, local(): pl.pallas_call(kernel, out_shape=jax.ShapeDtypeStruct(background_draws.sh...  45.6 us
    add x1, other arithmetic, local(): return background_draws + increments.astype(F32)  1.8 us

profile of v2, /device:TPU:1, one launch (start us, length us, event | category | flops | bytes accessed | tf_op | source)
XLA Modules:
  0.0 48.1 jit_solution(9233014909011698852)
XLA Ops:
  0.7 0.0 copy-start
  0.7 45.6 %shard_map.82 = bf16[4,32,1024]{2,1,0:T(8,128)(2,1)} custom-call(f32[4,32,1024]{2,1,0:T(8,128)} %bg_ref.1, bf16[4,32,1024]{2,1,0:T(8,128)(2,1)} %inn_ref.1, s32[1]{0:T(128)S(6)} %copy.9.tally_ref, s32[2,9]{1,0:T(2,128)} %kinds_ref.1, s32[4,1024]{1,0:T(4,128)} %constant.8.clone.region_ref, f32[2,64,128]{2,1,0:T(8,128)} %constant.9.clone.selfw_ref, ...), custom_call_target="tpu_custom_call" | custom-call | tf_op jit(solution)/shard_map/pallas_call | solution.py:424
  46.3 0.0 copy-done
  46.3 1.8 %convert_add_fusion = f32[4,32,1024]{2,1,0:T(8,128)} fusion(f32[4,32,1024]{2,1,0:T(8,128)S(1)} %copy-done, bf16[4,32,1024]{2,1,0:T(8,128)(2,1)} %shard_map.82), kind=kLoop, calls=%fused_computation | loop fusion | flops 262144 | bytes 1310720 | tf_op jit(solution)/shard_map/add | solution.py:472
Async XLA Ops:
  0.7 45.6 %copy-start = (f32[4,32,1024]{2,1,0:T(8,128)S(1)}, f32[4,32,1024]{2,1,0:T(8,128)}, u32[]{:S(2)}) copy-start(f32[4,32,1024]{2,1,0:T(8,128)} %bg_ref.1) | copy-start | bytes 1572868

commit v3 on v2

--- a/solution.py
+++ b/solution.py
@@ -13,7 +13,7 @@
 BF16 = jnp.bfloat16
 W = 8
 GROUPS = 16
-NEAR = [1, 15, 2, 14, 3, 13, 4, 12, 5, 11, 6, 10, 7, 9, 8]
+NEAR = [8, 9, 7, 10, 6, 11, 5, 12, 4, 13, 3, 14, 2, 15, 1]
 
 
 def taper_value(dy, dx):
@@ -61,21 +61,21 @@
             select[block, lane] = w * 128 + in_row * 16 + col
 
     for lane, (row, col, w) in enumerate(vert):
-        put(lane, 0, row, col, w)
-        put(384 + lane, 0, 5 + row, col, w)
-        put(lane, 1, 13 + row, col, w)
-        put(384 + lane, 1, 8 + row, col, w)
+        put(512 + lane, 0, row, col, w)
+        put(1024 + lane, 0, 5 + row, col, w)
+        put(512 + lane, 1, 13 + row, col, w)
+        put(1024 + lane, 1, 8 + row, col, w)
     for tile in range(3):
         for lane, (row, depth, w) in enumerate(sides[tile]):
             block = row // 8
-            at = 768 + (tile - block) * 128 + lane
+            at = (tile - block) * 128 + lane
             put(at, block, row, depth - 1, w)
             put(at + 256, block, row, 16 - depth, w)
     for lane, (a, b, w) in enumerate(corner):
-        put(1280 + lane, 0, a - 1, 16 - b, w)
-        put(1344 + lane, 0, a - 1, b - 1, w)
-        put(1280 + lane, 1, 16 - a, 16 - b, w)
-        put(1344 + lane, 1, 16 - a, b - 1, w)
+        put(896 + lane, 0, a - 1, 16 - b, w)
+        put(960 + lane, 0, a - 1, b - 1, w)
+        put(896 + lane, 1, 16 - a, 16 - b, w)
+        put(960 + lane, 1, 16 - a, b - 1, w)
 
     weights = np.zeros((4, 64, 1024), np.float32)
     kinds = np.full((4, 1024), 4, np.int32)
@@ -159,26 +159,18 @@
             ha[w, base + 32 : base + 40, :] = (d01 + d23) * 0.5
             ha[w, base + 48 : base + 56, :] = (d01 - d23) * 0.5
             hl[w, rows, :] = h0 - high
-    for w in range(W):
-        for m in range(4):
-            y = inn_ref[m, :, 128 * w : 128 * w + 128].astype(F32)
-            for r in range(4):
-                base = (r // 2) * 64 + m * 16 + (r % 2) * 8
-                hi[w, base : base + 8, :] = y[8 * r : 8 * r + 8, :]
-
-    def build(dest, carry):
-        col, core = dest // 2, dest % 2
+    def rows_of(source, dest, w):
+        return [source[w + n, pl.ds((dest % 2) * 64 + dest // 2, 8, stride=8), :] for n in range(2)]
+
+    def build_a(dest, carry):
         for w in range(0, W, 2):
-            for source, chunk in ((ha, ca), (hi, ci)):
-                a = source[w, pl.ds(core * 64 + col, 8, stride=8), :]
-                b = source[w + 1, pl.ds(core * 64 + col, 8, stride=8), :]
-                chunk[dest, 8 * w : 8 * w + 16, :] = jnp.concatenate([a, b], axis=0).astype(BF16)
+            ca[dest, 8 * w : 8 * w + 16, :] = jnp.concatenate(rows_of(ha, dest, w), axis=0).astype(BF16)
         for w in range(W):
-            stage[2 * w : 2 * w + 2, :] = hl[w, pl.ds(core * 16 + col, 2, stride=8), :]
+            stage[2 * w : 2 * w + 2, :] = hl[w, pl.ds((dest % 2) * 16 + dest // 2, 2, stride=8), :]
         ca[dest, 64:80, :] = stage[...].astype(BF16)
         return carry
 
-    lax.fori_loop(0, GROUPS, build, 0)
+    lax.fori_loop(0, GROUPS, build_a, 0)
 
     pl.semaphore_wait(barrier, GROUPS + 2)
 
@@ -214,6 +206,20 @@
         return copies
 
     a_copies = spread(ca, ra, as_, ar_)
+    for w in range(W):
+        for m in range(4):
+            y = inn_ref[m, :, 128 * w : 128 * w + 128].astype(F32)
+            for r in range(4):
+                base = (r // 2) * 64 + m * 16 + (r % 2) * 8
+                hi[w, base : base + 8, :] = y[8 * r : 8 * r + 8, :]
+
+
+    def build_i(dest, carry):
+        for w in range(0, W, 2):
+            ci[dest, 8 * w : 8 * w + 16, :] = jnp.concatenate(rows_of(hi, dest, w), axis=0).astype(BF16)
+        return carry
+
+    lax.fori_loop(0, GROUPS, build_i, 0)
     i_copies = spread(ci, ri, is_, ir_, 0, 64)
 
     for b in range(2):
@@ -226,53 +232,59 @@
 
         lax.fori_loop(0, 8, one_hot, 0)
 
-    def halo(hs, rh, send, recv):
-        plan = [
-            (UP, VDN, 384, (up_tile, 2 * z + other), 1),
-            (DN, VUP, 384, (down_tile, 2 * z + other), 0),
-            (TL, RIGHT, 384, (t, left + c), 3),
-            (TR, LEFT, 384, (t, right + c), 2),
-            (CU, CDL, 128, (up_tile, right + other), 6),
-            (CU, CDR, 128, (up_tile, left + other), 7),
-            (CD, CUL, 128, (down_tile, right + other), 4),
-            (CD, CUR, 128, (down_tile, left + other), 5),
-        ]
+    def halo(x, hs, rh, send, recv, inner_at):
         copies = []
-        for source, landing, width, device, n in plan:
+
+        def ship(source, landing, width, device, n):
             copy = pltpu.make_async_remote_copy(
                 src_ref=hs.at[:, source : source + width], dst_ref=rh.at[:, landing : landing + width],
                 send_sem=send.at[n], recv_sem=recv.at[n], device_id=device, device_id_type=MESH,
             )
             copy.start()
             copies.append(copy)
-        return copies
-
-    def pick(x, hs, inner_at):
-        m0 = jnp.dot(x[0], sel[0], preferred_element_type=F32)
-        m1 = jnp.dot(x[1], sel[1], preferred_element_type=F32)
-        hs[:, UP : UP + 384] = m0[:, 0:384].astype(BF16)
-        hs[:, DN : DN + 384] = m1[:, 0:384].astype(BF16)
+
+        def pick(b, start, stop):
+            return jnp.dot(x[b], sel[b, :, start:stop], preferred_element_type=F32)
+
+        m0, m1 = pick(0, 0, 512), pick(1, 0, 512)
         for k, place in enumerate((TL, TR)):
-            at0 = 768 + 256 * k
+            at0 = 256 * k
             hs[:, place : place + 128] = m0[:, at0 : at0 + 128].astype(BF16)
             hs[:, place + 128 : place + 256] = (m0[:, at0 + 128 : at0 + 256] + m1[:, at0 : at0 + 128]).astype(BF16)
             hs[:, place + 256 : place + 384] = m1[:, at0 + 128 : at0 + 256].astype(BF16)
-        hs[:, CU : CU + 128] = m0[:, 1280:1408].astype(BF16)
-        hs[:, CD : CD + 128] = m1[:, 1280:1408].astype(BF16)
-        inner[inner_at, 0] = m1[:, 384:768].astype(BF16)
-        inner[inner_at, 1] = m0[:, 384:768].astype(BF16)
-
-    def assemble(rh, ext, inner_at):
-        first = lax.broadcasted_iota(jnp.int32, (64, 128), 1) < 64
-        verts = (rh[:, VUP : VUP + 384], inner[inner_at, 0], inner[inner_at, 1], rh[:, VDN : VDN + 384])
-        above = jnp.where(first, rh[:, CUL : CUL + 128].astype(F32), rh[:, CUR : CUR + 128].astype(F32)).astype(BF16)
-        below = jnp.where(first, rh[:, CDL : CDL + 128].astype(F32), rh[:, CDR : CDR + 128].astype(F32)).astype(BF16)
+        ship(TL, RIGHT, 384, (t, left + c), 3)
+        ship(TR, LEFT, 384, (t, right + c), 2)
+        m0 = pick(0, 512, 1024).astype(BF16)
+        hs[:, UP : UP + 384] = m0[:, 0:384]
+        hs[:, CU : CU + 128] = m0[:, 384:512]
+        ship(CU, CDL, 128, (up_tile, right + other), 6)
+        ship(CU, CDR, 128, (up_tile, left + other), 7)
+        ship(UP, VDN, 384, (up_tile, 2 * z + other), 1)
+        m1 = pick(1, 512, 1024).astype(BF16)
+        hs[:, DN : DN + 384] = m1[:, 0:384]
+        hs[:, CD : CD + 128] = m1[:, 384:512]
+        ship(CD, CUL, 128, (down_tile, right + other), 4)
+        ship(CD, CUR, 128, (down_tile, left + other), 5)
+        ship(DN, VUP, 384, (down_tile, 2 * z + other), 0)
+        inner[inner_at, 0] = pick(1, 1024, 1408).astype(BF16)
+        inner[inner_at, 1] = pick(0, 1024, 1408).astype(BF16)
+        return copies
+
+    def sides(rh, ext, inner_at):
         for s in range(4):
             shift = 128 * (s // 2)
-            ext[s, :, 0:384] = verts[s]
-            ext[s, :, 384:512] = above if s < 2 else below
             ext[s, :, 512:768] = rh[:, LEFT + shift : LEFT + shift + 256]
             ext[s, :, 768:1024] = rh[:, RIGHT + shift : RIGHT + shift + 256]
+        for s in (1, 2):
+            ext[s, :, 0:384] = inner[inner_at, s - 1]
+            ext[s, :, 384:512] = jnp.zeros((64, 128), BF16)
+
+    def ends(rh, ext):
+        first = lax.broadcasted_iota(jnp.int32, (64, 128), 1) < 64
+        for s, vert, one, two in ((0, VUP, CUL, CUR), (3, VDN, CDL, CDR)):
+            ext[s, :, 0:384] = rh[:, vert : vert + 384]
+            corner = jnp.where(first, rh[:, one : one + 128].astype(F32), rh[:, two : two + 128].astype(F32))
+            ext[s, :, 384:512] = corner.astype(BF16)
 
     fa[pl.ds(pl.multiple_of(me * 80, 8), 80), :] = ca[me].astype(F32)
     for k in NEAR:
@@ -289,8 +301,7 @@
             parts += [fa[pl.ds(8 * w + 2 * m + b, 16, stride=80), :] for m in (1, 2, 3)]
             tile = jnp.concatenate(parts, axis=0) * land
             xa[b, :, lanes] = tile.astype(BF16)
-    pick(xa, hsa, 0)
-    ha_copies = halo(hsa, rha, hs_, hr_)
+    ha_copies = halo(xa, hsa, rha, hs_, hr_, 0)
 
     fi[pl.ds(pl.multiple_of(me * 64, 8), 64), :] = ci[me].astype(F32)
     for k in NEAR:
@@ -301,8 +312,7 @@
         for w in range(W):
             parts = [fi[pl.ds(8 * w + 2 * m + b, 16, stride=64), :] for m in range(4)]
             xi[b, :, 128 * w : 128 * w + 128] = jnp.concatenate(parts, axis=0).astype(BF16)
-    pick(xi, hsi, 1)
-    hi_copies = halo(hsi, rhi, gs_, gr_)
+    hi_copies = halo(xi, hsi, rhi, gs_, gr_, 1)
 
     for b in range(2):
         for w in range(W):
@@ -338,17 +348,18 @@
                 tt[s, 0, :, lanes] = part.reshape(512, 128).astype(BF16)
         return carry
 
-    lax.fori_loop(0, 4, own_taper, 0)
+    lax.fori_loop(0, 4, own_taper, 0, unroll=True)
     contract = (((1,), (1,)), ((), ()))
 
     def own_update(s, carry):
         acc[s] = lax.dot_general(tt[s, 0], xi[s // 2], contract, preferred_element_type=F32)
         return carry
 
-    lax.fori_loop(0, 4, own_update, 0)
+    lax.fori_loop(0, 4, own_update, 0, unroll=True)
     for copy in ha_copies:
         copy.wait_recv()
-    assemble(rha, exta, 0)
+    sides(rha, exta, 0)
+    ends(rha, exta)
 
     def halo_taper(s, carry):
         rows = at[s]
@@ -359,49 +370,68 @@
             tt[s, 1, :, lanes] = part.reshape(512, 256).astype(BF16)
         return carry
 
-    lax.fori_loop(0, 4, halo_taper, 0)
-
-    for copy in hi_copies:
-        copy.wait_recv()
-    assemble(rhi, exti, 1)
-
-    def halo_update(s, carry):
-        acc[s] = acc[s] + lax.dot_general(tt[s, 1], exti[s], contract, preferred_element_type=F32)
-        return carry
+    lax.fori_loop(0, 4, halo_taper, 0, unroll=True)
+
+    def halo_update(s, lanes):
+        acc[s] = acc[s] + lax.dot_general(tt[s, 1, :, lanes], exti[s, :, lanes], contract, preferred_element_type=F32)
 
     back = {}
-    for b in range(2):
-        lax.fori_loop(2 * b, 2 * b + 2, halo_update, 0)
-        for w in range(W):
-            rows = slice(64 * w, 64 * w + 64)
-            tile = jnp.concatenate([acc[2 * b, rows, :], acc[2 * b + 1, rows, :]], axis=0).T
-            at0 = (8 * b + w) * 64
-            rs[at0 : at0 + 64, :] = tile
-
-        def chunk(g, carry, b=b):
-            cb[g, b] = rs[pl.ds(512 * b + g, 32, stride=16), :].astype(BF16)
+
+    def give_back(phase, strips):
+        for n, s in enumerate(strips):
+            for p in range(4):
+                at0 = (8 * phase + 4 * n + p) * 64
+                rs[at0 : at0 + 64, :] = acc[s, 128 * p : 128 * p + 128, :].T
+
+        def chunk(g, carry):
+            cb[g, phase] = rs[pl.ds(512 * phase + g, 32, stride=16), :].astype(BF16)
             return carry
 
         lax.fori_loop(0, GROUPS, chunk, 0)
         for k in NEAR:
             peer = (me + k) % GROUPS
-            back[b, k] = pltpu.make_async_remote_copy(
-                src_ref=cb.at[peer, b], dst_ref=rb.at[me, b], send_sem=bs_.at[b, k], recv_sem=br_.at[b, k],
-                device_id=(t, peer), device_id_type=MESH,
+            back[phase, k] = pltpu.make_async_remote_copy(
+                src_ref=cb.at[peer, phase], dst_ref=rb.at[me, phase], send_sem=bs_.at[phase, k],
+                recv_sem=br_.at[phase, k], device_id=(t, peer), device_id_type=MESH,
             )
-            back[b, k].start()
-
-    for b in range(2):
-        fb[pl.ds(pl.multiple_of(me * 64 + 32 * b, 8), 32), :] = cb[me, b].astype(F32)
+            back[phase, k].start()
+
+    for copy in hi_copies[:2]:
+        copy.wait_recv()
+    sides(rhi, exti, 1)
+    for s in (1, 2):
+        halo_update(s, slice(0, 1024))
+    give_back(0, (1, 2))
+    for s in (0, 3):
+        halo_update(s, slice(512, 1024))
+    for copy in hi_copies[2:]:
+        copy.wait_recv()
+    ends(rhi, exti)
+    for s in (0, 3):
+        halo_update(s, slice(0, 512))
+    give_back(1, (0, 3))
+
+    for phase in range(2):
+        fb[pl.ds(pl.multiple_of(me * 64 + 32 * phase, 8), 32), :] = cb[me, phase].astype(F32)
         for k in NEAR:
-            back[b, k].wait_recv()
+            back[phase, k].wait_recv()
             g = (me + GROUPS - k) % GROUPS
-            fb[pl.ds(pl.multiple_of(g * 64 + 32 * b, 8), 32), :] = rb[g, b].astype(F32)
+            fb[pl.ds(pl.multiple_of(g * 64 + 32 * phase, 8), 32), :] = rb[g, phase].astype(F32)
+    first = lax.broadcasted_iota(jnp.int32, (8, 128), 1) < 64
+    place = (32, 0, 16, 48)
     for m in range(4):
         for core in range(2):
-            for w in range(W):
-                pair = [fb[pl.ds(core * 64 + b * 32 + 4 * w + m, 8, stride=128), :] for b in range(2)]
-                out_ref[m, 16 * core : 16 * core + 16, 128 * w : 128 * w + 128] = jnp.concatenate(pair, axis=0).astype(BF16)
+            rows = slice(16 * core, 16 * core + 16)
+            for p in range(4):
+                even, odd = [], []
+                for b in range(2):
+                    top, low = (
+                        fb[pl.ds(core * 64 + place[2 * b + n] + 4 * p + m, 8, stride=128), :] for n in range(2)
+                    )
+                    even.append(jnp.where(first, top, pltpu.roll(low, 64, 1)))
+                    odd.append(jnp.where(first, pltpu.roll(top, 64, 1), low))
+                for w, halves in ((2 * p, even), (2 * p + 1, odd)):
+                    out_ref[m, rows, 128 * w : 128 * w + 128] = jnp.concatenate(halves, axis=0).astype(BF16)
 
     for copies in (a_copies, i_copies, back):
         for copy in copies.values():

time: 48.2 us -> 45.1 us (0.936)
  Pallas kernels: 45.6 us -> 42.5 us
    pallas_call x1, Pallas kernels: 45.6 us -> 42.5 us  [local(): pl.pallas_call(kernel, out_shape=jax.ShapeDtypeStruct(background_draws.sh...]
where the time goes in v3:
time: 45.1 us; the launch traced here: 45 us
  Pallas kernels  42.5 us (94%)
  other arithmetic  1.8 us (4%)
  between operations  0.68 us (2%)
    pallas_call x1, Pallas kernels, local(): pl.pallas_call(kernel, out_shape=jax.ShapeDtypeStruct(background_draws.sh...  42.5 us
    add x1, other arithmetic, local(): return background_draws + increments.astype(F32)  1.8 us

profile of v3, /device:TPU:1, one launch (start us, length us, event | category | flops | bytes accessed | tf_op | source)
XLA Modules:
  0.0 45.0 jit_solution(8875993012470436317)
XLA Ops:
  0.7 0.0 copy-start
  0.7 42.5 %shard_map.82 = bf16[4,32,1024]{2,1,0:T(8,128)(2,1)} custom-call(f32[4,32,1024]{2,1,0:T(8,128)} %bg_ref.1, bf16[4,32,1024]{2,1,0:T(8,128)(2,1)} %inn_ref.1, s32[1]{0:T(128)S(6)} %copy.9.tally_ref, s32[2,9]{1,0:T(2,128)} %kinds_ref.1, s32[4,1024]{1,0:T(4,128)} %constant.8.clone.region_ref, f32[2,64,128]{2,1,0:T(8,128)} %constant.9.clone.selfw_ref, ...), custom_call_target="tpu_custom_call" | custom-call | tf_op jit(solution)/shard_map/pallas_call | solution.py:454
  43.1 0.0 copy-done
  43.1 1.8 %convert_add_fusion = f32[4,32,1024]{2,1,0:T(8,128)} fusion(f32[4,32,1024]{2,1,0:T(8,128)S(1)} %copy-done, bf16[4,32,1024]{2,1,0:T(8,128)(2,1)} %shard_map.82), kind=kLoop, calls=%fused_computation | loop fusion | flops 262144 | bytes 1310720 | tf_op jit(solution)/shard_map/add | solution.py:502
Async XLA Ops:
  0.7 42.5 %copy-start = (f32[4,32,1024]{2,1,0:T(8,128)S(1)}, f32[4,32,1024]{2,1,0:T(8,128)}, u32[]{:S(2)}) copy-start(f32[4,32,1024]{2,1,0:T(8,128)} %bg_ref.1) | copy-start | bytes 1572868

commit v4 on v3

--- a/solution.py
+++ b/solution.py
@@ -30,7 +30,7 @@
     return np.where(z <= 1, near, np.where(z < 2, far, 0)).astype(np.float32)
 
 
-def side_slots():
+def side_places():
     tiles = [[], [], []]
     for row in range(16):
         for depth in (1, 2, 3):
@@ -39,43 +39,35 @@
                 tile = 0
             if row == 10 and depth == 3:
                 tile = 2
-            tiles[tile] += [(row, depth, w) for w in range(W)]
+            tiles[tile].append((row, depth))
     return tiles
 
 
-def vert_slots():
-    return [(row, col, w) for w in range(W) for row in range(3) for col in range(16)]
-
-
-def corner_slots():
-    return [(a, b, w) for a in (1, 2, 3) for b in (1, 2, 3) if (a, b) != (3, 3) for w in range(W)]
+CORNER = [(a, b) for a in (1, 2, 3) for b in (1, 2, 3) if (a, b) != (3, 3)]
 
 
 def tables():
-    sides, vert, corner = side_slots(), vert_slots(), corner_slots()
-    select = np.full((2, 1408), -1, np.int32)
-
-    def put(lane, part, row, col, w):
-        block, in_row = divmod(row, 8)
-        if part is None or block == part:
-            select[block, lane] = w * 128 + in_row * 16 + col
-
-    for lane, (row, col, w) in enumerate(vert):
-        put(512 + lane, 0, row, col, w)
-        put(1024 + lane, 0, 5 + row, col, w)
-        put(512 + lane, 1, 13 + row, col, w)
-        put(1024 + lane, 1, 8 + row, col, w)
-    for tile in range(3):
-        for lane, (row, depth, w) in enumerate(sides[tile]):
-            block = row // 8
-            at = (tile - block) * 128 + lane
-            put(at, block, row, depth - 1, w)
-            put(at + 256, block, row, 16 - depth, w)
-    for lane, (a, b, w) in enumerate(corner):
-        put(896 + lane, 0, a - 1, 16 - b, w)
-        put(960 + lane, 0, a - 1, b - 1, w)
-        put(896 + lane, 1, 16 - a, 16 - b, w)
-        put(960 + lane, 1, 16 - a, b - 1, w)
+    sides = side_places()
+    select = np.full((2, 768), -1, np.int32)
+
+    def put(block, lane, row, col):
+        if row // 8 == block:
+            for w in range(4):
+                select[block, lane + w] = w * 128 + row % 8 * 16 + col
+
+    for block in range(2):
+        for k in range(2):
+            for n, (row, depth) in enumerate(sides[k + block]):
+                put(block, 64 * k + 4 * n, row, depth - 1)
+                put(block, 128 + 64 * k + 4 * n, row, 16 - depth)
+        for k in range(3):
+            for col in range(16):
+                put(block, 256 + 64 * k + 4 * col, 13 * block + k, col)
+                put(block, 512 + 64 * k + 4 * col, 5 + 3 * block + k, col)
+        for n, (a, b) in enumerate(CORNER):
+            row = 16 - a if block else a - 1
+            put(block, 448 + 4 * n, row, 16 - b)
+            put(block, 480 + 4 * n, row, b - 1)
 
     weights = np.zeros((4, 64, 1024), np.float32)
     kinds = np.full((4, 1024), 4, np.int32)
@@ -84,24 +76,25 @@
     for s in range(4):
         block = s // 2
         own_row, own_col = 4 * s + cell // 16, cell % 16
-        slots = [None] * 1024
-        base = [-3, 8, 5, 16][s]
-        for lane, (row, col, w) in enumerate(vert):
-            slots[lane] = (base + row, col)
+
+        def place(tile, n, row, col):
+            value = taper_value(row - own_row, col - own_col) / np.float32(63)
+            for quad in range(2):
+                lane = 128 * tile + 64 * quad + 4 * n
+                weights[s, :, lane : lane + 4] = value[:, None]
+                kinds[s, lane : lane + 4] = 3 * (row // 8 - block + 1) + col // 16 + 1
+
+        for k in range(3):
+            for col in range(16):
+                place(k, col, (-3, 8, 5, 16)[s] + k, col)
         if s in (0, 3):
-            for lane, (a, b, w) in enumerate(corner):
-                row = -a if s == 0 else 15 + a
-                slots[384 + lane] = (row, -b)
-                slots[448 + lane] = (row, 15 + b)
+            for n, (a, b) in enumerate(CORNER):
+                place(3, n, 15 + a if s else -a, -b)
+                place(3, 8 + n, 15 + a if s else -a, 15 + b)
         for k in range(2):
-            for lane, (row, depth, w) in enumerate(sides[k + (s >= 2)]):
-                slots[512 + 128 * k + lane] = (row, -depth)
-                slots[768 + 128 * k + lane] = (row, 15 + depth)
-        for lane, slot in enumerate(slots):
-            if slot is not None:
-                row, col = slot
-                weights[s, :, lane] = taper_value(row - own_row, col - own_col) / np.float32(63)
-                kinds[s, lane] = 3 * (row // 8 - block + 1) + col // 16 + 1
+            for n, (row, depth) in enumerate(sides[k + block]):
+                place(4 + k, n, row, -depth)
+                place(6 + k, n, row, 15 + depth)
         if s < 2:
             every = np.arange(128)
             self_weights[s] = taper_value(
@@ -226,48 +219,58 @@
         wanted = select_ref[b : b + 1, :]
 
         def one_hot(k, carry, b=b, wanted=wanted):
-            entry = lax.broadcasted_iota(jnp.int32, (128, 1408), 0) + 128 * k
+            entry = lax.broadcasted_iota(jnp.int32, (128, 768), 0) + 128 * k
             sel[b, pl.ds(pl.multiple_of(128 * k, 128), 128), :] = jnp.where(entry == wanted, 1.0, 0.0).astype(BF16)
             return carry
 
-        lax.fori_loop(0, 8, one_hot, 0)
-
-    def halo(x, hs, rh, send, recv, inner_at):
+        lax.fori_loop(0, 4, one_hot, 0)
+
+    lower = lane8 < 64
+
+    def halo(x, hs, rh, send, recv, inner_at, start, size):
+        rows = slice(start, start + size)
+        low = lax.broadcasted_iota(jnp.int32, (size, 128), 1) < 64
         copies = []
 
         def ship(source, landing, width, device, n):
             copy = pltpu.make_async_remote_copy(
-                src_ref=hs.at[:, source : source + width], dst_ref=rh.at[:, landing : landing + width],
+                src_ref=hs.at[rows, source : source + width], dst_ref=rh.at[rows, landing : landing + width],
                 send_sem=send.at[n], recv_sem=recv.at[n], device_id=device, device_id_type=MESH,
             )
             copy.start()
             copies.append(copy)
 
-        def pick(b, start, stop):
-            return jnp.dot(x[b], sel[b, :, start:stop], preferred_element_type=F32)
-
-        m0, m1 = pick(0, 0, 512), pick(1, 0, 512)
+        def pick(b, tiles):
+            first, last = 128 * tiles[0], 128 * tiles[-1] + 128
+            both = jnp.concatenate([x[b, rows, 0:512], x[b, rows, 512:1024]], axis=0)
+            found = jnp.dot(both, sel[b, :, first:last], preferred_element_type=F32)
+            out = []
+            for n in range(len(tiles)):
+                one, two = found[:size, 128 * n : 128 * n + 128], found[size:, 128 * n : 128 * n + 128]
+                out.append(jnp.where(low, one, pltpu.roll(two, 64, 1)))
+                out.append(jnp.where(low, pltpu.roll(one, 64, 1), two))
+            return out
+
+        def put(at0, tile):
+            hs[rows, at0 : at0 + 128] = tile.astype(BF16)
+
+        m0, m1 = pick(0, (0, 1)), pick(1, (0, 1))
         for k, place in enumerate((TL, TR)):
-            at0 = 256 * k
-            hs[:, place : place + 128] = m0[:, at0 : at0 + 128].astype(BF16)
-            hs[:, place + 128 : place + 256] = (m0[:, at0 + 128 : at0 + 256] + m1[:, at0 : at0 + 128]).astype(BF16)
-            hs[:, place + 256 : place + 384] = m1[:, at0 + 128 : at0 + 256].astype(BF16)
+            put(place, m0[2 * k])
+            put(place + 128, m0[2 * k + 1] + m1[2 * k])
+            put(place + 256, m1[2 * k + 1])
         ship(TL, RIGHT, 384, (t, left + c), 3)
         ship(TR, LEFT, 384, (t, right + c), 2)
-        m0 = pick(0, 512, 1024).astype(BF16)
-        hs[:, UP : UP + 384] = m0[:, 0:384]
-        hs[:, CU : CU + 128] = m0[:, 384:512]
-        ship(CU, CDL, 128, (up_tile, right + other), 6)
-        ship(CU, CDR, 128, (up_tile, left + other), 7)
-        ship(UP, VDN, 384, (up_tile, 2 * z + other), 1)
-        m1 = pick(1, 512, 1024).astype(BF16)
-        hs[:, DN : DN + 384] = m1[:, 0:384]
-        hs[:, CD : CD + 128] = m1[:, 384:512]
-        ship(CD, CUL, 128, (down_tile, right + other), 4)
-        ship(CD, CUR, 128, (down_tile, left + other), 5)
-        ship(DN, VUP, 384, (down_tile, 2 * z + other), 0)
-        inner[inner_at, 0] = pick(1, 1024, 1408).astype(BF16)
-        inner[inner_at, 1] = pick(0, 1024, 1408).astype(BF16)
+        for b, vert, corner in ((0, UP, CU), (1, DN, CD)):
+            found = pick(b, (2, 3, 4, 5))
+            for n in range(3):
+                put(vert + 128 * n, found[n])
+                inner[inner_at, 1 - b, rows, 128 * n : 128 * n + 128] = found[4 + n].astype(BF16)
+            put(corner, found[3])
+            tile = down_tile if b else up_tile
+            ship(corner, CUL if b else CDL, 128, (tile, right + other), 4 if b else 6)
+            ship(corner, CUR if b else CDR, 128, (tile, left + other), 5 if b else 7)
+            ship(vert, VUP if b else VDN, 384, (tile, 2 * z + other), 0 if b else 1)
         return copies
 
     def sides(rh, ext, inner_at):
@@ -280,11 +283,29 @@
             ext[s, :, 384:512] = jnp.zeros((64, 128), BF16)
 
     def ends(rh, ext):
-        first = lax.broadcasted_iota(jnp.int32, (64, 128), 1) < 64
+        first = lax.broadcasted_iota(jnp.int32, (64, 128), 1) % 64 < 32
         for s, vert, one, two in ((0, VUP, CUL, CUR), (3, VDN, CDL, CDR)):
             ext[s, :, 0:384] = rh[:, vert : vert + 384]
             corner = jnp.where(first, rh[:, one : one + 128].astype(F32), rh[:, two : two + 128].astype(F32))
             ext[s, :, 384:512] = corner.astype(BF16)
+
+    load_weight.wait()
+    for b in range(2):
+        @pl.when(4 * (2 * c + b) + z // 2 != me)
+        def _(b=b):
+            pltpu.make_async_remote_copy(
+                src_ref=mask_out.at[0], dst_ref=mask_in.at[b], send_sem=mask_send.at[0], recv_sem=mask_recv.at[b],
+                device_id=(t, (me + 1) % GROUPS), device_id_type=MESH,
+            ).wait_recv()
+
+    for s in range(4):
+        block = s // 2
+        region = region_ref[s : s + 1, :]
+        row = jnp.zeros((1, 1024), F32)
+        for k in ((0, 1, 2, 3, 5), (3, 5, 6, 7, 8), (0, 1, 2, 3, 5), (3, 5, 6, 7, 8))[s]:
+            row = jnp.where(region == k, mask_in[block, 0:1, k : k + 1], row)
+        weight[s] = weight[s] * row
+
 
     fa[pl.ds(pl.multiple_of(me * 80, 8), 80), :] = ca[me].astype(F32)
     for k in NEAR:
@@ -301,42 +322,13 @@
             parts += [fa[pl.ds(8 * w + 2 * m + b, 16, stride=80), :] for m in (1, 2, 3)]
             tile = jnp.concatenate(parts, axis=0) * land
             xa[b, :, lanes] = tile.astype(BF16)
-    ha_copies = halo(xa, hsa, rha, hs_, hr_, 0)
-
-    fi[pl.ds(pl.multiple_of(me * 64, 8), 64), :] = ci[me].astype(F32)
-    for k in NEAR:
-        i_copies[k].wait_recv()
-        g = (me + GROUPS - k) % GROUPS
-        fi[pl.ds(pl.multiple_of(g * 64, 8), 64), :] = ri[g].astype(F32)
-    for b in range(2):
-        for w in range(W):
-            parts = [fi[pl.ds(8 * w + 2 * m + b, 16, stride=64), :] for m in range(4)]
-            xi[b, :, 128 * w : 128 * w + 128] = jnp.concatenate(parts, axis=0).astype(BF16)
-    hi_copies = halo(xi, hsi, rhi, gs_, gr_, 1)
+    ha_copies = halo(xa, hsa, rha, hs_, hr_, 0, 0, 64)
 
     for b in range(2):
         for w in range(W):
             turned = xa[b, :, 128 * w : 128 * w + 128].astype(F32).T.astype(BF16)
             at[2 * b, 64 * w : 64 * w + 64, :] = turned[0:64]
             at[2 * b + 1, 64 * w : 64 * w + 64, :] = turned[64:128]
-    load_weight.wait()
-    for b in range(2):
-        @pl.when(4 * (2 * c + b) + z // 2 != me)
-        def _(b=b):
-            pltpu.make_async_remote_copy(
-                src_ref=mask_out.at[0], dst_ref=mask_in.at[b], send_sem=mask_send.at[0], recv_sem=mask_recv.at[b],
-                device_id=(t, (me + 1) % GROUPS), device_id_type=MESH,
-            ).wait_recv()
-
-    for s in range(4):
-        block = s // 2
-        region = region_ref[s : s + 1, :]
-        row = jnp.zeros((1, 1024), F32)
-        for k in ((0, 1, 2, 3, 5), (3, 5, 6, 7, 8), (0, 1, 2, 3, 5), (3, 5, 6, 7, 8))[s]:
-            row = jnp.where(region == k, mask_in[block, 0:1, k : k + 1], row)
-        weight[s] = weight[s] * row
-
-
     def own_taper(s, carry):
         rows = at[s]
         table = selfw_ref[s % 2]
@@ -349,17 +341,27 @@
         return carry
 
     lax.fori_loop(0, 4, own_taper, 0, unroll=True)
+    fi[pl.ds(pl.multiple_of(me * 64, 8), 64), :] = ci[me].astype(F32)
+    for k in NEAR:
+        i_copies[k].wait_recv()
+        g = (me + GROUPS - k) % GROUPS
+        fi[pl.ds(pl.multiple_of(g * 64, 8), 64), :] = ri[g].astype(F32)
+    for b in range(2):
+        for w in range(W):
+            parts = [fi[pl.ds(8 * w + 2 * m + b, 16, stride=64), :] for m in range(4)]
+            xi[b, :, 128 * w : 128 * w + 128] = jnp.concatenate(parts, axis=0).astype(BF16)
+    hi_copies = halo(xi, hsi, rhi, gs_, gr_, 1, 0, 64)
+
     contract = (((1,), (1,)), ((), ()))
 
     def own_update(s, carry):
-        acc[s] = lax.dot_general(tt[s, 0], xi[s // 2], contract, preferred_element_type=F32)
+        acc[s] = lax.dot_general(xi[s // 2], tt[s, 0], contract, preferred_element_type=F32)
         return carry
 
     lax.fori_loop(0, 4, own_update, 0, unroll=True)
-    for copy in ha_copies:
+    for copy in ha_copies[:2]:
         copy.wait_recv()
     sides(rha, exta, 0)
-    ends(rha, exta)
 
     def halo_taper(s, carry):
         rows = at[s]
@@ -370,10 +372,16 @@
             tt[s, 1, :, lanes] = part.reshape(512, 256).astype(BF16)
         return carry
 
-    lax.fori_loop(0, 4, halo_taper, 0, unroll=True)
+    for s in (1, 2):
+        halo_taper(s, 0)
+    for copy in ha_copies[2:]:
+        copy.wait_recv()
+    ends(rha, exta)
+    for s in (0, 3):
+        halo_taper(s, 0)
 
     def halo_update(s, lanes):
-        acc[s] = acc[s] + lax.dot_general(tt[s, 1, :, lanes], exti[s, :, lanes], contract, preferred_element_type=F32)
+        acc[s] = acc[s] + lax.dot_general(exti[s, :, lanes], tt[s, 1, :, lanes], contract, preferred_element_type=F32)
 
     back = {}
 
@@ -381,13 +389,13 @@
         for n, s in enumerate(strips):
             for p in range(4):
                 at0 = (8 * phase + 4 * n + p) * 64
-                rs[at0 : at0 + 64, :] = acc[s, 128 * p : 128 * p + 128, :].T
+                rs[at0 : at0 + 64, :] = acc[s, :, 128 * p : 128 * p + 128]
 
         def chunk(g, carry):
             cb[g, phase] = rs[pl.ds(512 * phase + g, 32, stride=16), :].astype(BF16)
             return carry
 
-        lax.fori_loop(0, GROUPS, chunk, 0)
+        lax.fori_loop(0, GROUPS, chunk, 0, unroll=4)
         for k in NEAR:
             peer = (me + k) % GROUPS
             back[phase, k] = pltpu.make_async_remote_copy(
@@ -457,7 +465,7 @@
         in_specs=[vmem, vmem, pl.BlockSpec(memory_space=pltpu.SMEM), vmem, vmem, vmem, vmem, anywhere],
         out_specs=vmem,
         scratch_shapes=[
-            pltpu.VMEM((2, 1024, 1408), BF16),
+            pltpu.VMEM((2, 512, 768), BF16),
             pltpu.VMEM((4, 64, 1024), F32),
             pltpu.VMEM((2, 8, 128), F32),
             pltpu.VMEM((2, 8, 128), F32),
@@ -482,7 +490,7 @@
             pltpu.VMEM((4, 64, 1024), BF16),
             pltpu.VMEM((4, 64, 1024), BF16),
             pltpu.VMEM((4, 2, 512, 1024), BF16),
-            pltpu.VMEM((4, 512, 64), F32),
+            pltpu.VMEM((4, 64, 512), F32),
             pltpu.VMEM((1024, 128), F32),
             pltpu.VMEM((GROUPS, 2, 32, 128), BF16),
             pltpu.VMEM((GROUPS, 2, 32, 128), BF16),

time: 45.1 us -> 44.4 us (0.984)
  Pallas kernels: 42.5 us -> 41.8 us
    pallas_call x1, Pallas kernels: 42.5 us -> 41.8 us  [local(): pl.pallas_call(kernel, out_shape=jax.ShapeDtypeStruct(background_draws.sh...]
where the time goes in v4:
time: 44.4 us; the launch traced here: 44.3 us
  Pallas kernels  41.8 us (94%)
  other arithmetic  1.8 us (4%)
  between operations  0.68 us (2%)
    pallas_call x1, Pallas kernels, local(): pl.pallas_call(kernel, out_shape=jax.ShapeDtypeStruct(background_draws.sh...  41.8 us
    add x1, other arithmetic, local(): return background_draws + increments.astype(F32)  1.8 us

profile of v4, /device:TPU:1, one launch (start us, length us, event | category | flops | bytes accessed | tf_op | source)
XLA Modules:
  0.0 44.3 jit_solution(17946415815233731717)
XLA Ops:
  0.7 0.0 copy-start
  0.7 41.8 %shard_map.82 = bf16[4,32,1024]{2,1,0:T(8,128)(2,1)} custom-call(f32[4,32,1024]{2,1,0:T(8,128)} %bg_ref.1, bf16[4,32,1024]{2,1,0:T(8,128)(2,1)} %inn_ref.1, s32[1]{0:T(128)S(6)} %copy.9.tally_ref, s32[2,9]{1,0:T(2,128)} %kinds_ref.1, s32[4,1024]{1,0:T(4,128)} %constant.8.clone.region_ref, f32[2,64,128]{2,1,0:T(8,128)} %constant.9.clone.selfw_ref, ...), custom_call_target="tpu_custom_call" | custom-call | tf_op jit(solution)/shard_map/pallas_call | solution.py:462
  42.4 0.0 copy-done
  42.4 1.8 %convert_add_fusion = f32[4,32,1024]{2,1,0:T(8,128)} fusion(f32[4,32,1024]{2,1,0:T(8,128)S(1)} %copy-done, bf16[4,32,1024]{2,1,0:T(8,128)(2,1)} %shard_map.82), kind=kLoop, calls=%fused_computation | loop fusion | flops 262144 | bytes 1310720 | tf_op jit(solution)/shard_map/add | solution.py:510
Async XLA Ops:
  0.7 41.8 %copy-start = (f32[4,32,1024]{2,1,0:T(8,128)S(1)}, f32[4,32,1024]{2,1,0:T(8,128)}, u32[]{:S(2)}) copy-start(f32[4,32,1024]{2,1,0:T(8,128)} %bg_ref.1) | copy-start | bytes 1572868

commit v5 on v4

--- a/solution.py
+++ b/solution.py
@@ -254,13 +254,6 @@
         def put(at0, tile):
             hs[rows, at0 : at0 + 128] = tile.astype(BF16)
 
-        m0, m1 = pick(0, (0, 1)), pick(1, (0, 1))
-        for k, place in enumerate((TL, TR)):
-            put(place, m0[2 * k])
-            put(place + 128, m0[2 * k + 1] + m1[2 * k])
-            put(place + 256, m1[2 * k + 1])
-        ship(TL, RIGHT, 384, (t, left + c), 3)
-        ship(TR, LEFT, 384, (t, right + c), 2)
         for b, vert, corner in ((0, UP, CU), (1, DN, CD)):
             found = pick(b, (2, 3, 4, 5))
             for n in range(3):
@@ -271,6 +264,13 @@
             ship(corner, CUL if b else CDL, 128, (tile, right + other), 4 if b else 6)
             ship(corner, CUR if b else CDR, 128, (tile, left + other), 5 if b else 7)
             ship(vert, VUP if b else VDN, 384, (tile, 2 * z + other), 0 if b else 1)
+        m0, m1 = pick(0, (0, 1)), pick(1, (0, 1))
+        for k, place in enumerate((TL, TR)):
+            put(place, m0[2 * k])
+            put(place + 128, m0[2 * k + 1] + m1[2 * k])
+            put(place + 256, m1[2 * k + 1])
+        ship(TL, RIGHT, 384, (t, left + c), 3)
+        ship(TR, LEFT, 384, (t, right + c), 2)
         return copies
 
     def sides(rh, ext, inner_at):
@@ -359,7 +359,7 @@
         return carry
 
     lax.fori_loop(0, 4, own_update, 0, unroll=True)
-    for copy in ha_copies[:2]:
+    for copy in ha_copies[6:]:
         copy.wait_recv()
     sides(rha, exta, 0)
 
@@ -374,7 +374,7 @@
 
     for s in (1, 2):
         halo_taper(s, 0)
-    for copy in ha_copies[2:]:
+    for copy in ha_copies[:6]:
         copy.wait_recv()
     ends(rha, exta)
     for s in (0, 3):
@@ -404,7 +404,7 @@
             )
             back[phase, k].start()
 
-    for copy in hi_copies[:2]:
+    for copy in hi_copies[6:]:
         copy.wait_recv()
     sides(rhi, exti, 1)
     for s in (1, 2):
@@ -412,7 +412,7 @@
     give_back(0, (1, 2))
     for s in (0, 3):
         halo_update(s, slice(512, 1024))
-    for copy in hi_copies[2:]:
+    for copy in hi_copies[:6]:
         copy.wait_recv()
     ends(rhi, exti)
     for s in (0, 3):

time: 44.4 us -> 43.8 us (0.986)
  Pallas kernels: 41.8 us -> 41.2 us
    pallas_call x1, Pallas kernels: 41.8 us -> 41.2 us  [local(): pl.pallas_call(kernel, out_shape=jax.ShapeDtypeStruct(background_draws.sh...]
where the time goes in v5:
time: 43.8 us; the launch traced here: 43.6 us
  Pallas kernels  41.2 us (94%)
  other arithmetic  1.8 us (4%)
  between operations  0.68 us (2%)
    pallas_call x1, Pallas kernels, local(): pl.pallas_call(kernel, out_shape=jax.ShapeDtypeStruct(background_draws.sh...  41.2 us
    add x1, other arithmetic, local(): return background_draws + increments.astype(F32)  1.8 us

profile of v5, /device:TPU:1, one launch (start us, length us, event | category | flops | bytes accessed | tf_op | source)
XLA Modules:
  0.0 43.6 jit_solution(11958319457712535744)
XLA Ops:
  0.7 0.0 copy-start
  0.7 41.2 %shard_map.82 = bf16[4,32,1024]{2,1,0:T(8,128)(2,1)} custom-call(f32[4,32,1024]{2,1,0:T(8,128)} %bg_ref.1, bf16[4,32,1024]{2,1,0:T(8,128)(2,1)} %inn_ref.1, s32[1]{0:T(128)S(6)} %copy.9.tally_ref, s32[2,9]{1,0:T(2,128)} %kinds_ref.1, s32[4,1024]{1,0:T(4,128)} %constant.8.clone.region_ref, f32[2,64,128]{2,1,0:T(8,128)} %constant.9.clone.selfw_ref, ...), custom_call_target="tpu_custom_call" | custom-call | tf_op jit(solution)/shard_map/pallas_call | solution.py:462
  41.8 0.0 copy-done
  41.8 1.8 %convert_add_fusion = f32[4,32,1024]{2,1,0:T(8,128)} fusion(f32[4,32,1024]{2,1,0:T(8,128)S(1)} %copy-done, bf16[4,32,1024]{2,1,0:T(8,128)(2,1)} %shard_map.82), kind=kLoop, calls=%fused_computation | loop fusion | flops 262144 | bytes 1310720 | tf_op jit(solution)/shard_map/add | solution.py:510
Async XLA Ops:
  0.7 41.2 %copy-start = (f32[4,32,1024]{2,1,0:T(8,128)S(1)}, f32[4,32,1024]{2,1,0:T(8,128)}, u32[]{:S(2)}) copy-start(f32[4,32,1024]{2,1,0:T(8,128)} %bg_ref.1) | copy-start | bytes 1572868
